TPU v7x, 256 devices: a whole 4x4x8 slice. The times are simulated.
256 devices in a mesh: group: 2 (over z_lo), row: 16 (over z_hi, x), col: 8 (over y, core).
Axes of the slice: x: 4, y: 4, z: 8 (z_hi: 4, z_lo: 2; z = z_hi * 2 + z_lo), core: 2. Of those that a mesh axis runs over, the one named last changes fastest.
Arguments:
- student_image: bfloat16 [32768, 768], P(('group', 'row', 'col')), may hold values from -32 to 32
- student_proj: bfloat16 [768, 512], replicated, may hold values from -1.1 to 1.1
- student_text: bfloat16 [32768, 512], P(('group', 'row', 'col')), may hold values from -4 to 4
- teacher_image: bfloat16 [32768, 1664], P(('group', 'col'), 'row'), may hold values from -32 to 32
- teacher_proj: bfloat16 [1664, 1280], P('row', 'col'), may hold values from -1.1 to 1.1
- teacher_text: bfloat16 [32768, 1280], P(('group', 'row', 'col')), may hold values from -4 to 4
- assignment: int32 [2, 16384], P('group', ('row', 'col')), may hold values from 0 to 16383, as said below
- pair_ids: int32 [2, 16384], P('group', ('row', 'col')), may hold values from 0 to 16383, each once within a row
Outputs:
- grad_embed: float32 [32768, 512], P(('group', 'row', 'col'))
- grad_proj: float32 [768, 512], replicated
Inputs may be any that keep to these rules, and one draw needn't show every extreme that they name: `assignment`: within each sub-batch a permutation. The slots of the device at row r, col c of the layout take only teacher indices c * 16 * 128 to (c + 1) * 16 * 128 - 1, and exactly 8 of them from each run of 128 teacher indices there. `pair_ids`: each row a permutation.
All inputs are finite; a program needn't handle non-finite values.
Results may differ from a plain program's by a relative error of at most 0.0078.
Values may be sent and summed in bfloat16 or wider, within the bound.
A program may use at most 128 MiB of HBM per device.

v0:
```python
import math

import jax
import jax.numpy as jnp
from jax import lax
from jax.sharding import PartitionSpec as P

logit_scale = 100.0
norm_eps = 1e-06


def combined_all(part, axis, combine):
    gathered = jax.tree.map(lambda a: lax.all_gather(a, axis), part)

    def take(source):
        return jax.tree.map(lambda a: lax.dynamic_index_in_dim(a, source, 0, False), gathered)

    return lax.fori_loop(
        1, lax.axis_size(axis), lambda source, state: combine(state, take(source)), take(0)
    )


def unit_rows(values):
    return values * lax.rsqrt(jnp.sum(values * values, axis=1, keepdims=True) + norm_eps)


def merge_stats(earlier, later):
    merged = []
    for position in range(0, len(earlier), 2):
        highest = jnp.maximum(earlier[position], later[position])
        combined = earlier[position + 1] * jnp.exp(earlier[position] - highest) + later[
            position + 1
        ] * jnp.exp(later[position] - highest)
        merged += [highest, combined]
    return tuple(merged)


def tile_scores(images, texts):
    return logit_scale * jnp.einsum("ik,jk->ij", images, texts, preferred_element_type=jnp.float32)


def row_partial(values):
    highest = jnp.max(values, axis=1)
    return (highest, jnp.sum(jnp.exp(values - highest[:, None]), axis=1))


def column_partial(values):
    highest = jnp.max(values, axis=0)
    return (highest, jnp.sum(jnp.exp(values - highest[None, :]), axis=0))


def log_totals(stats):
    return (stats[0] + jnp.log(stats[1]), stats[2] + jnp.log(stats[3]))


def source_rows(order, per_device, column_block):
    return order % column_block // per_device


def slot_ranks(sources):
    slots = jnp.arange(sources.shape[-1], dtype=jnp.int32)
    earlier = slots[None, :] < slots[:, None]
    same_source = sources[..., :, None] == sources[..., None, :]
    return jnp.sum(same_source & earlier, axis=-1)


def body(
    student_image,
    student_proj,
    student_text,
    teacher_image,
    teacher_proj,
    teacher_text,
    assignment,
    pair_ids,
):
    row_devices = lax.axis_size("row")
    per_device = student_image.shape[0]
    share_rows = per_device // row_devices
    column_block = per_device * row_devices
    proj_rows = lax.all_gather(teacher_proj, "col", axis=1, tiled=True)
    teacher_raw = lax.psum_scatter(
        jnp.dot(teacher_image, proj_rows, preferred_element_type=jnp.float32),
        "row",
        scatter_dimension=0,
        tiled=True,
    )
    teacher_embed = unit_rows(teacher_raw).astype(jnp.bfloat16)
    own_order = assignment[0]
    column_order = lax.all_gather(own_order, "row", axis=0, tiled=True).reshape(
        row_devices, per_device
    )
    column_sources = source_rows(column_order, per_device, column_block)
    column_ranks = slot_ranks(column_sources)
    own_row = lax.axis_index("row")
    share_slots = jnp.arange(share_rows, dtype=jnp.int32)
    wanted = (column_sources == own_row)[:, :, None] & (
        column_ranks[:, :, None] == share_slots[None, None, :]
    )
    picked = jnp.sum(jnp.where(wanted, (column_order % per_device)[:, :, None], 0), axis=1)
    outgoing = teacher_embed[picked.reshape(-1)].reshape(
        row_devices, share_rows, teacher_embed.shape[1]
    )
    incoming = lax.all_to_all(outgoing, "row", split_axis=0, concat_axis=0, tiled=True)
    own_sources = source_rows(own_order, per_device, column_block)
    relaid = incoming.reshape(row_devices * share_rows, -1)[
        own_sources * share_rows + slot_ranks(own_sources)
    ]
    raw_student = jnp.dot(student_image, student_proj, preferred_element_type=jnp.float32)
    student_unit = unit_rows(raw_student)
    student_embed = student_unit.astype(jnp.bfloat16)
    text_unit = unit_rows(student_text.astype(jnp.float32)).astype(jnp.bfloat16)
    teacher_unit = unit_rows(teacher_text.astype(jnp.float32)).astype(jnp.bfloat16)
    image_student, image_teacher = (
        lax.all_gather(student_embed, "col", axis=0, tiled=True),
        lax.all_gather(relaid, "col", axis=0, tiled=True),
    )
    image_pairs = lax.all_gather(pair_ids[0], "col", axis=0, tiled=True)
    text_student, text_teacher = (
        lax.all_gather(text_unit, "row", axis=0, tiled=True),
        lax.all_gather(teacher_unit, "row", axis=0, tiled=True),
    )
    text_slots = jnp.arange(text_student.shape[0], dtype=jnp.int32)
    text_ids = (
        text_slots // per_device * lax.axis_size("col") + lax.axis_index("col")
    ) * per_device + text_slots % per_device
    tile_rows = image_student.shape[0]
    block_rows = math.gcd(tile_rows, 512)
    block_starts = list(range(0, tile_rows, block_rows))
    teacher_blocks = []
    row_parts = []
    column_stats = None
    for start in block_starts:
        student_scores = tile_scores(image_student[start : start + block_rows], text_student)
        teacher_scores = tile_scores(image_teacher[start : start + block_rows], text_teacher)
        teacher_blocks.append(teacher_scores)
        row_parts.append(row_partial(student_scores) + row_partial(teacher_scores))
        block_columns = column_partial(student_scores) + column_partial(teacher_scores)
        column_stats = (
            block_columns if column_stats is None else merge_stats(column_stats, block_columns)
        )
    row_local = tuple(
        (
            jnp.concatenate([partial_stats[position] for partial_stats in row_parts])
            for position in range(4)
        )
    )
    row_stats = combined_all(row_local, "col", merge_stats)
    column_totals = combined_all(column_stats, "row", merge_stats)
    student_row, teacher_row = log_totals(row_stats)
    student_col, teacher_col = log_totals(column_totals)
    groups = lax.axis_size("group")
    partial_grads = []
    for position, start in enumerate(block_starts):
        student_scores = tile_scores(image_student[start : start + block_rows], text_student)
        teacher_scores = teacher_blocks[position]
        srow = student_row[start : start + block_rows]
        trow = teacher_row[start : start + block_rows]
        matched = (image_pairs[start : start + block_rows][:, None] == text_ids[None, :]).astype(
            jnp.float32
        )
        weights = (
            2.0 * jnp.exp(student_scores - srow[:, None])
            + 2.0 * jnp.exp(student_scores - student_col[None, :])
            - jnp.exp(teacher_scores - trow[:, None])
            - jnp.exp(teacher_scores - teacher_col[None, :])
            - 2.0 * matched
        ) / groups
        partial_grads.append(
            logit_scale
            * jnp.dot(
                weights.astype(jnp.bfloat16), text_student, preferred_element_type=jnp.float32
            )
        )
    embed_grad = lax.psum_scatter(
        jnp.concatenate(partial_grads, 0), "col", scatter_dimension=0, tiled=True
    )
    inner_term = jnp.sum(student_unit * embed_grad, axis=1, keepdims=True)
    grad_embed = (embed_grad - student_unit * inner_term) * lax.rsqrt(
        jnp.sum(raw_student * raw_student, axis=1, keepdims=True) + norm_eps
    )
    weight_partial = jnp.dot(
        student_image.T, grad_embed.astype(jnp.bfloat16), preferred_element_type=jnp.float32
    )
    grad_proj = lax.psum(weight_partial, ("group", "row", "col"))
    return (grad_embed, grad_proj)


def solution(mesh):
    placed = (
        P(("group", "row", "col"), None),
        P(),
        P(("group", "row", "col"), None),
        P(("group", "col"), "row"),
        P("row", "col"),
        P(("group", "row", "col"), None),
        P("group", ("row", "col")),
        P("group", ("row", "col")),
    )
    return jax.shard_map(
        body,
        mesh=mesh,
        in_specs=placed,
        out_specs=(P(("group", "row", "col"), None), P()),
        check_vma=False,
    )
```

profile of v0, /device:TPU:1, one launch (start us, length us, event | category | flops | bytes accessed | tf_op | source)
XLA Modules:
  0.0 799.5 jit_solution(8456506162695655426)
XLA Ops:
  8.1 16.3 %all_gather.67 = bf16[104,1280]{0,1:T(8,128)(2,1)S(1)} all-gather(bf16[104,160]{0,1:T(8,128)(2,1)} %param.16), channel_id=1, replica_groups=mesh['group'=2,'row'=16,'col'=8] {'col'}, dimensions={1}, use_global_device_ids=true | all-gather | bytes 299520 | tf_op jit(solution)/shard_map/all_gather | solution.py:81
  24.4 6.6 fusion.46
  31.1 0.8 copy-done.9
  31.9 0.3 multiply_reduce_fusion.2
  32.3 0.8 multiply_convert_fusion.9
  33.2 0.8 fusion.11
  34.1 0.1 fusion.6
  34.2 0.9 fusion.7
  35.1 40.8 %all-gather.2 = s32[1,2048]{1,0:T(1,128)S(1)} all-gather(s32[1,128]{1,0:T(1,128)S(1)} %copy-done.15), channel_id=4, replica_groups=mesh['group'=2,'row'=16,'col'=8] {'row'}, dimensions={1}, use_global_device_ids=true | all-gather | bytes 8704 | tf_op jit(solution)/shard_map/all_gather | solution.py:90
  75.9 0.6 convert_reduce_fusion
  76.6 0.3 select_reduce_fusion
  77.1 121.8 %reduce-scatter.3.cloned.1.call-done = f32[128,1280]{1,0:T(8,128)} async-done(((f32[2048,1280]{1,0:T(8,128)}), f32[128,1280]{1,0:T(8,128)}) %reduce-scatter.3.cloned.1.call-update) | async-done | bytes 655376 | tf_op jit(solution)/shard_map/reduce_scatter | solution.py:82
  198.9 1.2 multiply_reduce_fusion
  200.1 1.2 multiply_convert_fusion.8
  201.3 1.6 gather_fusion
  202.9 7.1 all-to-all-start
  210.1 0.2 convert_reduce_fusion.1
  210.3 19.0 %all-to-all-done = bf16[16,8,1280]{2,1,0:T(8,128)(2,1)S(1)} async-done(((bf16[16,8,1280]{2,1,0:T(8,128)(2,1)}), bf16[16,8,1280]{2,1,0:T(8,128)(2,1)S(1)}, u32[]{:S(2)}, u32[]{:S(2)}) %all-to-all-start) | async-done | bytes 327712 | tf_op jit(solution)/shard_map/all_to_all | solution.py:104
  229.3 1.6 gather_fusion.1
  231.0 12.1 %all-gather.6 = s32[1,1024]{1,0:T(1,128)S(1)} all-gather(s32[1,128]{1,0:T(1,128)S(1)} %copy-done.16), channel_id=8, replica_groups=mesh['group'=2,'row'=16,'col'=8] {'col'}, dimensions={1}, use_global_device_ids=true | all-gather | bytes 4608 | tf_op jit(solution)/shard_map/all_gather | solution.py:118
  243.2 3.3 fusion.41
  246.5 1.4 fusion.42
  247.9 0.5 copy-done.1
  248.5 2.7 exponential_reduce_fusion.2
  251.2 41.3 %all-gather.7 = f32[16,1,2048]{2,1,0:T(1,128)S(1)} all-gather(f32[1,1,2048]{2,1,0:T(1,128)S(1)} %get-tuple-element.533), channel_id=1, replica_groups=mesh['group'=2,'row'=16,'col'=8] {'row'}, dimensions={0}, use_global_device_ids=true | all-gather | bytes 139264 | tf_op jit(solution)/shard_map/all_gather | solution.py:13
  292.5 31.8 %all-gather.8 = f32[16,1,2048]{2,1,0:T(1,128)S(1)} all-gather(f32[1,1,2048]{2,1,0:T(1,128)S(1)} %get-tuple-element.532), channel_id=1, replica_groups=mesh['group'=2,'row'=16,'col'=8] {'row'}, dimensions={0}, use_global_device_ids=true | all-gather | bytes 139264 | tf_op jit(solution)/shard_map/all_gather | solution.py:13
  324.4 25.9 %all-gather.1 = f32[8192]{0:T(1024)S(1)} all-gather(f32[1024]{0:T(1024)S(1)} %pad_maximum_fusion.2), channel_id=3, replica_groups=mesh['group'=2,'row'=16,'col'=8] {'col'}, dimensions={0}, use_global_device_ids=true | all-gather | bytes 36864 | tf_op jit(solution)/shard_map/all_gather | solution.py:13
  350.3 13.0 %all-gather = f32[8192]{0:T(1024)S(1)} all-gather(f32[1024]{0:T(1024)S(1)} %pad_maximum_fusion.1), channel_id=2, replica_groups=mesh['group'=2,'row'=16,'col'=8] {'col'}, dimensions={0}, use_global_device_ids=true | all-gather | bytes 36864 | tf_op jit(solution)/shard_map/all_gather | solution.py:13
  363.4 5.6 fusion.40
  369.1 3.0 fusion.39
  372.1 2.7 exponential_reduce_fusion
  374.9 33.4 %all-gather.9 = f32[16,1,2048]{2,1,0:T(1,128)S(1)} all-gather(f32[1,1,2048]{2,1,0:T(1,128)S(1)} %get-tuple-element.531), channel_id=1, replica_groups=mesh['group'=2,'row'=16,'col'=8] {'row'}, dimensions={0}, use_global_device_ids=true | all-gather | bytes 139264 | tf_op jit(solution)/shard_map/all_gather | solution.py:13
  408.3 32.1 %all-gather.10 = f32[16,1,2048]{2,1,0:T(1,128)S(1)} all-gather(f32[1,1,2048]{2,1,0:T(1,128)S(1)} %get-tuple-element.530), channel_id=1, replica_groups=mesh['group'=2,'row'=16,'col'=8] {'row'}, dimensions={0}, use_global_device_ids=true | all-gather | bytes 139264 | tf_op jit(solution)/shard_map/all_gather | solution.py:13
  440.5 26.7 %all-gather.5 = f32[8192]{0:T(1024)S(1)} all-gather(f32[1024]{0:T(1024)S(1)} %pad_maximum_fusion.4), channel_id=7, replica_groups=mesh['group'=2,'row'=16,'col'=8] {'col'}, dimensions={0}, use_global_device_ids=true | all-gather | bytes 36864 | tf_op jit(solution)/shard_map/all_gather | solution.py:13
  467.2 12.8 %all-gather.4 = f32[8192]{0:T(1024)S(1)} all-gather(f32[1024]{0:T(1024)S(1)} %pad_maximum_fusion.3), channel_id=6, replica_groups=mesh['group'=2,'row'=16,'col'=8] {'col'}, dimensions={0}, use_global_device_ids=true | all-gather | bytes 36864 | tf_op jit(solution)/shard_map/all_gather | solution.py:13
  480.1 2.1 while.43
  482.2 0.8 while.42
  483.2 6.2 fusion.3
  489.4 0.2 copy-done.5
  489.7 0.6 copy-done.20
  490.2 3.1 fusion.2
  493.3 1.5 pad_maximum_fusion
  494.9 31.1 %reduce-scatter.5.cloned.1.call-done = f32[128,512]{1,0:T(8,128)} async-done(((f32[1024,512]{1,0:T(8,128)}), f32[128,512]{1,0:T(8,128)}) %reduce-scatter.5.cloned.1.call-update) | async-done | bytes 262160 | tf_op jit(solution)/shard_map/reduce_scatter | solution.py:175
  526.0 1.1 multiply_reduce_fusion.1
  527.1 1.1 subtract_multiply_fusion
  528.2 1.5 convolution_bitcast_fusion
  529.7 259.2 %all-reduce.2.cloned.1.call-done = f32[768,512]{0,1:T(8,128)} async-done(((f32[768,512]{0,1:T(8,128)}), f32[768,512]{0,1:T(8,128)}) %all-reduce.2.cloned.1.call-update) | async-done | bytes 1572880 | tf_op jit(solution)/shard_map/psum | solution.py:185
  788.9 3.0 copy.13
  (217 shorter events, 3.0 us)
Async XLA Ops:
  8.0 23.1 %copy-start = (bf16[768,512]{1,0:T(8,128)(2,1)S(1)}, bf16[768,512]{1,0:T(8,128)(2,1)}, u32[]{:S(2)}) copy-start(bf16[768,512]{1,0:T(8,128)(2,1)} %param.13) | copy-start | bytes 2359300
  8.0 190.9 %reduce-scatter.3.cloned.1.call-start = ((), (), s32[]{:S(2)}) async-start(), calls=%async_computation.5 | async-start | bytes 11141120 | tf_op jit(solution)/shard_map/reduce_scatter | solution.py:82
  31.0 0.9 copy-start.9
  31.0 2.1 copy-start.12
  31.0 3.1 copy-start.7
  31.0 4.1 copy-start.15
  31.0 212.2 %all-gather.16.cloned.1.call-start = ((), (), s32[]{:S(2)}) async-start(), calls=%async_computation.3 | async-start | bytes 1179648 | tf_op jit(solution)/shard_map/all_gather | solution.py:115
  33.0 210.2 %all-gather.18.cloned.1.call-start = ((), (), s32[]{:S(2)}) async-start(), calls=%async_computation.4 | async-start | bytes 2228224 | tf_op jit(solution)/shard_map/all_gather | solution.py:120
  34.0 329.4 %all-gather.20.cloned.1.call-start = ((), (), s32[]{:S(2)}) async-start(), calls=%async_computation.6 | async-start | bytes 5570560 | tf_op jit(solution)/shard_map/all_gather | solution.py:121
  77.1 153.9 %copy-start.16 = (s32[1,128]{1,0:T(1,128)S(1)}, s32[1,128]{1,0:T(1,128)}, u32[]{:S(2)}) copy-start(s32[1,128]{1,0:T(1,128)} %param.19) | copy-start | bytes 1540
  202.9 26.4 %all-to-all-start = ((bf16[16,8,1280]{2,1,0:T(8,128)(2,1)}), bf16[16,8,1280]{2,1,0:T(8,128)(2,1)S(1)}, u32[]{:S(2)}, u32[]{:S(2)}) async-start(bf16[16,8,1280]{2,1,0:T(8,128)(2,1)} %bitcast.10), calls=%async_computation.1 | async-start | bytes 655360 | tf_op jit(solution)/shard_map/all_to_all | solution.py:104
  210.0 153.4 %all-gather.22.cloned.1.call-start = ((), (), s32[]{:S(2)}) async-start(), calls=%async_computation.9 | async-start | bytes 2949120 | tf_op jit(solution)/shard_map/all_gather | solution.py:116
  231.0 295.0 %reduce-scatter.5.cloned.1.call-start = ((), (), s32[]{:S(2)}) async-start(), calls=%async_computation.7 | async-start | bytes 2359296 | tf_op jit(solution)/shard_map/reduce_scatter | solution.py:175
  243.2 3.3 copy-start.21
  243.2 3.3 copy-start.19
  246.5 1.9 copy-start.1
  247.9 3.2 copy-start.3
  292.4 76.6 %copy-start.10 = (f32[16,1,2048]{2,1,0:T(1,128)}, f32[16,1,2048]{2,1,0:T(1,128)S(1)}, u32[]{:S(2)}) copy-start(f32[16,1,2048]{2,1,0:T(1,128)S(1)} %all-gather.7) | copy-start | bytes 393220
  324.3 44.7 %copy-start.11 = (f32[16,1,2048]{2,1,0:T(1,128)}, f32[16,1,2048]{2,1,0:T(1,128)S(1)}, u32[]{:S(2)}) copy-start(f32[16,1,2048]{2,1,0:T(1,128)S(1)} %all-gather.8) | copy-start | bytes 393220
  350.3 18.7 %copy-start.13 = (f32[8192]{0:T(1024)}, f32[8192]{0:T(1024)S(1)}, u32[]{:S(2)}) copy-start(f32[8192]{0:T(1024)S(1)} %all-gather.1) | copy-start | bytes 98308
  363.3 5.7 copy-start.14
  363.4 5.6 copy-start.17
  363.4 5.6 copy-start.18
  369.1 3.0 copy-start.6
  372.1 2.8 copy-start.4
  372.1 108.0 %slice-start = ((f32[16,1,2048]{2,1,0:T(1,128)}), f32[1,1,2048]{2,1,0:T(1,128)S(1)}, s32[]{:S(2)}) async-start(f32[16,1,2048]{2,1,0:T(1,128)} %copy-done.10), calls=%async_computation.10 | async-start | bytes 16384 | tf_op jit(solution)/shard_map/jit(dynamic_index_in_dim)/dynamic_slice | solution.py:16
  372.1 108.0 %slice-start.1 = ((f32[16,1,2048]{2,1,0:T(1,128)}), f32[1,1,2048]{2,1,0:T(1,128)S(1)}, s32[]{:S(2)}) async-start(f32[16,1,2048]{2,1,0:T(1,128)} %copy-done.11), calls=%async_computation.11 | async-start | bytes 16384 | tf_op jit(solution)/shard_map/jit(dynamic_index_in_dim)/dynamic_slice | solution.py:16
  372.1 110.1 %slice-start.2 = ((f32[8192]{0:T(1024)}), f32[1024]{0:T(1024)S(1)}, s32[]{:S(2)}) async-start(f32[8192]{0:T(1024)} %copy-done.13), calls=%async_computation.12 | async-start | bytes 8192 | tf_op jit(solution)/shard_map/jit(dynamic_index_in_dim)/dynamic_slice | solution.py:16
  372.1 110.1 %slice-start.3 = ((f32[8192]{0:T(1024)}), f32[1024]{0:T(1024)S(1)}, s32[]{:S(2)}) async-start(f32[8192]{0:T(1024)} %copy-done.14), calls=%async_computation.13 | async-start | bytes 8192 | tf_op jit(solution)/shard_map/jit(dynamic_index_in_dim)/dynamic_slice | solution.py:16
  483.1 6.3 copy-start.2
  483.1 6.5 copy-start.5
  483.1 7.1 copy-start.20
  494.9 294.0 %all-reduce.2.cloned.1.call-start = ((), (), s32[]{:S(2)}) async-start(), calls=%async_computation.8 | async-start | bytes 3145728 | tf_op jit(solution)/shard_map/psum | solution.py:185
  528.2 263.8 %copy-start.8 = (f32[128,512]{1,0:T(8,128)}, f32[128,512]{1,0:T(8,128)S(1)}, u32[]{:S(2)}) copy-start(f32[128,512]{1,0:T(8,128)S(1)} %subtract_multiply_fusion) | copy-start | bytes 786436
Sparse Core Ops, SparseCore 0:
  31.1 167.7 reduce-scatter.2
  529.9 259.0 all-reduce.1
Sparse Core Ops, SparseCore 1:
  33.4 26.7 all-gather.15
  63.0 87.7 all-gather.17
  153.6 109.9 all-gather.19
  265.4 27.5 all-gather.21
  495.0 31.0 reduce-scatter.4
where the time goes:
time: 801 us; the launch traced here: 800 us
  waiting for transfers between devices  431 us (54%)
  blocking collectives  286 us (36%)
  matrix products  31 us (4%)
  between operations  16.3 us (2%)
  other arithmetic  15.9 us (2%)
  local copies, waits for them, and re-layouts  10.2 us (1%)
    psum x1, waiting for transfers between devices, body(): grad_proj = lax.psum(weight_partial, ('group', 'row', 'col'))  259 us
    all_gather x8, blocking collectives, combined_all(): gathered = jax.tree.map(lambda a: lax.all_gather(a, axis), part)  217 us
    reduce_scatter x1, waiting for transfers between devices, body(): lax.psum_scatter(jnp.dot(teacher_image, proj_rows, preferred_element_type...  122 us
    all_gather x1, blocking collectives, body(): lax.all_gather(own_order, 'row', axis=0, tiled=True)  40.8 us
    reduce_scatter x1, waiting for transfers between devices, body(): lax.psum_scatter(jnp.concatenate(partial_grads, 0), 'col', scatter_dimens...  31.1 us
    all_to_all x1, waiting for transfers between devices, body(): lax.all_to_all(outgoing, 'row', split_axis=0, concat_axis=0, tiled=True)  19 us
    all_gather x1, blocking collectives, body(): proj_rows = lax.all_gather(teacher_proj, 'col', axis=1, tiled=True)  16.3 us
  transfers between devices with their start and end apart: 8, of which 4 were waited for; matrix products, arithmetic and copies ran while one was open for 2% of the time, Pallas kernels for 0%

commit v1 on v0

v1 whole, which is shorter than its diff:
```python
import math

import jax
import jax.numpy as jnp
from jax import lax
from jax.experimental import pallas as pl
from jax.experimental.pallas import tpu as pltpu
from jax.sharding import PartitionSpec as P

logit_scale = 100.0
score_scale = logit_scale * math.log2(math.e)
lowest = -1e30
norm_eps = 1e-06
MESH = pl.DeviceIdType.MESH
ring = 4
n_row = 16
n_col = 8
nt_dims = (((1,), (1,)), ((), ()))
tn_dims = (((0,), (0,)), ((), ()))


def unit_rows(values):
    return values * lax.rsqrt(jnp.sum(values * values, axis=1, keepdims=True) + norm_eps)


class Place:
    def __init__(self):
        self.row = lax.axis_index("row")
        self.col = lax.axis_index("col")
        self.z, self.x = self.row // ring, self.row % ring
        self.y, self.core = self.col // 2, self.col % 2

    def along_x(self, step):
        return (self.x + step + ring) % ring

    def along_y(self, step):
        return (self.y + step + ring) % ring

    def along_z(self, step):
        return (self.z + step + ring) % ring

    def to_x(self, step):
        return {"row": self.z * ring + self.along_x(step)}

    def to_z(self, step):
        return {"row": self.along_z(step) * ring + self.x}

    def to_y(self, step):
        return {"col": self.along_y(step) * 2 + self.core}

    def sibling(self):
        return {"col": self.y * 2 + 1 - self.core}


class Mail:
    def __init__(self, send_sem, recv_sem):
        self.send_sem, self.recv_sem = send_sem, recv_sem
        self.used = 0
        self.sent = []

    def push(self, src, dst, device):
        index = self.used
        self.used += 1
        copy = pltpu.make_async_remote_copy(
            src_ref=src,
            dst_ref=dst,
            send_sem=self.send_sem.at[index],
            recv_sem=self.recv_sem.at[index],
            device_id=device,
            device_id_type=MESH,
        )
        copy.start()
        self.sent.append(copy)
        return index, device

    def got(self, slot, ticket):
        index, device = ticket
        pltpu.make_async_remote_copy(
            src_ref=slot,
            dst_ref=slot,
            send_sem=self.send_sem.at[index],
            recv_sem=self.recv_sem.at[index],
            device_id=device,
            device_id_type=MESH,
        ).wait_recv()

    def finish(self):
        for copy in self.sent:
            copy.wait_send()


def all_peers(place):
    return (
        [{"row": (place.row + step) % n_row} for step in range(1, n_row)]
        + [{"col": (place.col + step) % n_col} for step in range(1, n_col)]
        + [{"group": 1 - lax.axis_index("group")}]
    )


class AlongColumn:
    def __init__(self, mail, place, ref):
        self.mail, self.place, self.ref = mail, place, ref
        self.half = ref.shape[1] // 2

    def block(self, step, core):
        return self.place.along_y(step) * 2 + core

    def lower(self, index):
        return self.ref.at[index, pl.ds(0, self.half)]

    def upper(self, index):
        return self.ref.at[index, pl.ds(self.half, self.half)]

    def start(self):
        place, mail = self.place, self.mail
        own = self.ref.at[place.col]
        self.up = mail.push(own, own, place.to_y(1))
        self.down = mail.push(own, own, place.to_y(-1))
        self.over = [mail.push(own, own, place.sibling())]

    def forward(self):
        place, mail = self.place, self.mail
        below = self.block(-1, place.core)
        mail.got(self.ref.at[below], self.up)
        self.up_half = mail.push(self.lower(below), self.lower(below), place.to_y(1))
        self.over.append(mail.push(self.ref.at[below], self.ref.at[below], place.sibling()))
        above = self.block(1, place.core)
        mail.got(self.ref.at[above], self.down)
        self.down_half = mail.push(self.upper(above), self.upper(above), place.to_y(-1))
        self.over.append(mail.push(self.ref.at[above], self.ref.at[above], place.sibling()))

    def last(self):
        place, mail = self.place, self.mail
        far = self.block(2, place.core)
        mail.got(self.lower(far), self.up_half)
        self.over.append(mail.push(self.lower(far), self.lower(far), place.sibling()))
        mail.got(self.upper(far), self.down_half)
        self.over.append(mail.push(self.upper(far), self.upper(far), place.sibling()))

    def end(self):
        place, mail = self.place, self.mail
        other = 1 - place.core
        mail.got(self.ref.at[self.block(0, other)], self.over[0])
        mail.got(self.ref.at[self.block(-1, other)], self.over[1])
        mail.got(self.ref.at[self.block(1, other)], self.over[2])
        far = self.block(2, other)
        mail.got(self.lower(far), self.over[3])
        mail.got(self.upper(far), self.over[4])


def step_kernel(
    si_hbm,
    sp_hbm,
    st_hbm,
    ti_hbm,
    pt_hbm,
    tt_hbm,
    order_hbm,
    pair_hbm,
    embed_out,
    proj_out,
    si_ref,
    sp_ref,
    st_ref,
    ti_ref,
    tt_ref,
    text,
    img_s,
    img_t,
    pairs,
    raw_ref,
    orders,
    feat_out,
    feat_in,
    proj,
    embed,
    scores,
    row_high,
    row_total,
    col_high,
    col_total,
    row_stats,
    row_landed,
    row_lse,
    col_stats,
    col_landed,
    col_lse,
    row_tiles,
    offsets,
    partial_grad,
    from_core,
    leaving,
    arriving,
    partial,
    from_sibling,
    summed,
    first_in,
    second,
    second_in,
    third,
    third_in,
    fourth,
    fourth_in,
    load_sem,
    send_sem,
    recv_sem,
):
    place = Place()
    mail = Mail(send_sem, recv_sem)
    row, col, core = place.row, place.col, place.core
    other = 1 - core
    per_device, width = st_ref.shape
    teacher_width = tt_ref.shape[1]
    half = per_device // 2

    loads = []
    for source, target in (
        (order_hbm, orders.at[row]),
        (pt_hbm, proj.at[col, row]),
        (pair_hbm, pairs.at[col]),
        (st_hbm, st_ref),
        (tt_hbm, tt_ref),
        (si_hbm, si_ref),
        (sp_hbm, sp_ref),
        (ti_hbm, ti_ref),
    ):
        copy = pltpu.make_async_copy(source, target, load_sem.at[len(loads)])
        copy.start()
        loads.append(copy)
    barrier = pltpu.get_barrier_semaphore()
    peers = all_peers(place)
    for device in peers:
        pl.semaphore_signal(barrier, inc=1, device_id=device, device_id_type=MESH)
    for copy in loads[:5]:
        copy.wait()
    own_x, own_z = place.x, place.z
    text[own_x, own_z, :, :teacher_width] = unit_rows(tt_ref[...].astype(jnp.float32)).astype(
        jnp.bfloat16
    )
    text[own_x, own_z, :, teacher_width:] = unit_rows(st_ref[...].astype(jnp.float32)).astype(
        jnp.bfloat16
    )
    pl.semaphore_wait(barrier, len(peers))

    own_order = orders.at[row]
    order_mail = [
        mail.push(own_order, own_order, {"row": (row + step) % n_row}) for step in range(1, n_row)
    ]
    own_proj = proj.at[col, row]
    proj_x = [mail.push(own_proj, own_proj, place.to_x(step)) for step in (1, 3, 2)]

    def block(dx, dz, part):
        return text.at[place.along_x(dx), place.along_z(dz), pl.ds(part * half, half)]

    z_up, z_down, x_up, x_down, x_on = {}, {}, {}, {}, {}

    def start_z(part):
        z_up[part] = mail.push(block(0, 0, part), block(0, 0, part), place.to_z(1))
        z_down[part] = mail.push(block(0, 0, part), block(0, 0, part), place.to_z(-1))

    def start_x(dz, part):
        x_up[dz, part] = mail.push(block(0, dz, part), block(0, dz, part), place.to_x(1))
        x_down[dz, part] = mail.push(block(0, dz, part), block(0, dz, part), place.to_x(-1))

    def forward_x(dz):
        mail.got(block(-1, dz, 0), x_up[dz, 0])
        x_on[dz, 0] = mail.push(block(-1, dz, 0), block(-1, dz, 0), place.to_x(1))
        mail.got(block(1, dz, 1), x_down[dz, 1])
        x_on[dz, 1] = mail.push(block(1, dz, 1), block(1, dz, 1), place.to_x(-1))

    start_z(0)
    start_x(0, 0)
    start_x(0, 1)
    loads[5].wait()
    loads[6].wait()
    raw_student = jnp.dot(si_ref[...], sp_ref[...], preferred_element_type=jnp.float32)
    raw_ref[...] = raw_student
    img_s[col] = unit_rows(raw_student).astype(jnp.bfloat16)
    student = AlongColumn(mail, place, img_s)
    student.start()
    own_pairs = pairs.at[col]
    pair_mail = [
        mail.push(own_pairs, own_pairs, {"col": (col + step) % n_col}) for step in range(1, n_col)
    ]
    for step, ticket in zip((1, 3, 2), proj_x):
        mail.got(proj.at[col, place.z * ring + place.along_x(-step)], ticket)

    def proj_rows(step):
        return proj.at[col, pl.ds(place.along_z(step) * ring, ring)]

    proj_z = [mail.push(proj_rows(0), proj_rows(0), place.to_z(step)) for step in (1, 3, 2)]
    start_z(1)

    loads[7].wait()
    for step in range(1, n_row):
        mail.got(orders.at[(row + n_row - step) % n_row], order_mail[step - 1])
    lanes = lax.broadcasted_iota(jnp.int32, (per_device, 2 * per_device), 1).astype(jnp.float32)

    def pick(target, carry):
        wanted = (orders[target] - col * (n_row * per_device)).astype(jnp.float32)
        wanted = jnp.broadcast_to(wanted, (per_device, per_device)).T
        wanted = jnp.concatenate([wanted, wanted], axis=1)
        total = jnp.zeros((per_device, ti_ref.shape[0]), jnp.float32)
        for start in range(0, n_row * per_device, 2 * per_device):
            chosen = jnp.where(wanted == lanes + float(start), 1.0, 0.0).astype(jnp.bfloat16)
            total += lax.dot_general(
                chosen,
                ti_ref[:, start : start + 2 * per_device],
                nt_dims,
                preferred_element_type=jnp.float32,
            )
        feat_out[target] = total.astype(jnp.bfloat16)
        return carry

    lax.fori_loop(0, n_row, pick, 0)
    feat_mail = []
    for step in range(1, n_row):
        target = (row + step) % n_row
        feat_mail.append(mail.push(feat_out.at[target], feat_in.at[row], {"row": target}))
    feat_in[row] = feat_out[row]

    mail.got(block(0, -1, 0), z_up[0])
    z_up_on = mail.push(block(0, -1, 0), block(0, -1, 0), place.to_z(1))
    start_x(-1, 0)
    mail.got(block(0, 1, 0), z_down[0])
    start_x(1, 0)
    student.forward()
    forward_x(0)
    for step, ticket in zip((1, 3, 2), proj_z):
        mail.got(proj_rows(-step), ticket)
    gathered_proj = AlongColumn(mail, place, proj)
    gathered_proj.start()
    mail.got(block(0, 1, 1), z_down[1])
    z_down_on = mail.push(block(0, 1, 1), block(0, 1, 1), place.to_z(-1))
    start_x(1, 1)
    mail.got(block(0, -1, 1), z_up[1])
    start_x(-1, 1)
    student.last()
    gathered_proj.forward()
    mail.got(block(0, 2, 0), z_up_on)
    start_x(2, 0)
    mail.got(block(0, 2, 1), z_down_on)
    start_x(2, 1)
    gathered_proj.last()
    gathered_proj.end()
    for step in range(1, n_row):
        mail.got(feat_in.at[(row + n_row - step) % n_row], feat_mail[step - 1])
    proj_width = proj.shape[2]

    def project(source, carry):
        total = jnp.zeros((proj_width, per_device), jnp.float32)
        for features in range(n_row):
            total += lax.dot_general(
                proj[source, features],
                feat_in[features],
                nt_dims,
                preferred_element_type=jnp.float32,
            )
        embed[pl.ds(pl.multiple_of(source * proj_width, 8), proj_width), :] = total
        return carry

    lax.fori_loop(0, n_col, project, 0)
    raw_teacher = embed[...]
    scale = lax.rsqrt(jnp.sum(raw_teacher * raw_teacher, axis=0, keepdims=True) + norm_eps)
    img_t[col] = (raw_teacher * scale).T.astype(jnp.bfloat16)
    teacher = AlongColumn(mail, place, img_t)
    teacher.start()
    student.end()
    forward_x(-1)
    teacher.forward()
    forward_x(1)
    teacher.last()
    for step in range(1, n_col):
        mail.got(pairs.at[(col + n_col - step) % n_col], pair_mail[step - 1])
    slot = lax.broadcasted_iota(jnp.int32, (per_device, per_device), 1)
    for source in range(n_col):
        wide = jnp.broadcast_to(pairs[source].astype(jnp.float32), (per_device, per_device)).T
        offsets[source * per_device : (source + 1) * per_device] = wide.astype(jnp.int32) - slot
    row_high[...] = jnp.full(row_high.shape, lowest, jnp.float32)
    row_total[...] = jnp.zeros(row_total.shape, jnp.float32)
    teacher.end()

    image_rows = 2 * per_device
    chunk = ring * per_device
    col_mail = {}

    def text_student(index):
        return text[index, :, :, teacher_width:].reshape(chunk, width)

    def text_teacher(index):
        return text[index, :, :, :teacher_width].reshape(chunk, teacher_width)

    def process(dx):
        index = place.along_x(dx)
        col_high[...] = jnp.full(col_high.shape, lowest, jnp.float32)
        col_total[...] = jnp.zeros(col_total.shape, jnp.float32)

        def images(step, carry):
            rows = pl.ds(pl.multiple_of(step * image_rows, image_rows), image_rows)
            for kind in range(2):
                if kind == 0:
                    left = img_s[pl.ds(2 * step, 2)].reshape(image_rows, width)
                    right = text_student(index)
                else:
                    left = img_t[pl.ds(2 * step, 2)].reshape(image_rows, teacher_width)
                    right = text_teacher(index)
                values = score_scale * lax.dot_general(
                    left, right, nt_dims, preferred_element_type=jnp.float32
                )
                scores[kind, index, rows] = values
                tiles = [
                    values[:, start : start + per_device] for start in range(0, chunk, per_device)
                ]
                before = row_high[kind, rows]
                high = before
                for tile in tiles:
                    high = jnp.maximum(high, tile)
                total = row_total[kind, rows] * jnp.exp2(before - high)
                for tile in tiles:
                    total = total + jnp.exp2(tile - high)
                row_high[kind, rows] = high
                row_total[kind, rows] = total
                stacked = values.reshape(image_rows // 8, 8, chunk)
                before = col_high[kind]
                high = jnp.maximum(before, jnp.max(stacked, axis=0))
                total = col_total[kind] * jnp.exp2(before - high)
                col_total[kind] = total + jnp.sum(jnp.exp2(stacked - high[None]), axis=0)
                col_high[kind] = high
            return carry

        lax.fori_loop(0, ring, images, 0)
        found = []
        for kind in range(2):
            high = jnp.max(col_high[kind], axis=0, keepdims=True)
            total = jnp.sum(
                col_total[kind] * jnp.exp2(col_high[kind] - high), axis=0, keepdims=True
            )
            found += [high, total]
        found = jnp.concatenate(found + [jnp.zeros((4, chunk), jnp.float32)], axis=0)
        for z in range(ring):
            col_stats[index, z] = found[:, z * per_device : (z + 1) * per_device]
        for dz in range(ring):
            z = place.along_z(dz)
            if dx or dz:
                col_mail[dx, dz] = mail.push(
                    col_stats.at[index, z],
                    col_landed.at[own_x, own_z],
                    {"row": z * ring + index},
                )
            else:
                col_landed[own_x, own_z] = col_stats[index, z]

    process(0)
    forward_x(2)
    for dx, part, tickets in ((-1, 1, x_up), (1, 0, x_down)):
        for dz in (0, -1, 1, 2):
            mail.got(block(dx, dz, part), tickets[dz, part])
        process(dx % ring)
    for part in range(2):
        for dz in (0, -1, 1, 2):
            mail.got(block(2, dz, part), x_on[dz, part])
    process(2)

    for source in range(n_col):
        rows = slice(source * per_device, (source + 1) * per_device)
        found = []
        for kind in range(2):
            high_all = row_high[kind, rows].T
            high = jnp.max(high_all, axis=0, keepdims=True)
            total = jnp.sum(
                row_total[kind, rows].T * jnp.exp2(high_all - high), axis=0, keepdims=True
            )
            found += [high, total]
        row_stats[source] = jnp.concatenate(
            found + [jnp.zeros((4, per_device), jnp.float32)], axis=0
        )
    row_mail = [
        mail.push(
            row_stats.at[(col + step) % n_col],
            row_landed.at[col],
            {"col": (col + step) % n_col},
        )
        for step in range(1, n_col)
    ]
    row_landed[col] = row_stats[col]

    def merge(parts):
        found = []
        for kind in range(2):
            high = jnp.max(parts[:, 2 * kind], axis=0, keepdims=True)
            total = jnp.sum(
                parts[:, 2 * kind + 1] * jnp.exp2(parts[:, 2 * kind] - high),
                axis=0,
                keepdims=True,
            )
            found.append(high + jnp.log2(total) + float(kind))
        return jnp.concatenate(found + [jnp.zeros((6, per_device), jnp.float32)], axis=0)

    pairs_of_steps = [(dx, dz) for dx in range(ring) for dz in range(ring) if dx or dz]
    for dx, dz in pairs_of_steps:
        mail.got(col_landed.at[place.along_x(-dx), place.along_z(-dz)], col_mail[dx, dz])
    col_lse[own_x, own_z] = merge(col_landed[...].reshape(n_row, 8, per_device))
    own_lse = col_lse.at[own_x, own_z]
    col_back = {
        (dx, dz): mail.push(
            own_lse, own_lse, {"row": place.along_z(dz) * ring + place.along_x(dx)}
        )
        for dx, dz in pairs_of_steps
    }
    for step in range(1, n_col):
        mail.got(row_landed.at[(col + n_col - step) % n_col], row_mail[step - 1])
    row_lse[col] = merge(row_landed[...])
    row_back = [
        mail.push(row_lse.at[col], row_lse.at[col], {"col": (col + step) % n_col})
        for step in range(1, n_col)
    ]
    for step in range(1, n_col):
        mail.got(row_lse.at[(col + n_col - step) % n_col], row_back[step - 1])
    for source in range(n_col):
        rows = slice(source * per_device, (source + 1) * per_device)
        for kind in range(2):
            wide = row_lse[source, kind : kind + 1, :]
            row_tiles[kind, rows] = jnp.broadcast_to(wide, (per_device, per_device)).T
    for dx, dz in pairs_of_steps:
        mail.got(col_lse.at[place.along_x(-dx), place.along_z(-dz)], col_back[dx, dz])

    over = {}
    across = {}

    def weigh(step):
        target = place.along_y(step)
        rows = pl.ds(pl.multiple_of(target * image_rows, image_rows), image_rows)
        partial_grad[target] = jnp.zeros(partial_grad.shape[1:], jnp.float32)

        def texts(index, carry):
            parts = []
            for z in range(ring):
                lane = slice(z * per_device, (z + 1) * per_device)
                student_scores = scores[0, index, rows, lane]
                teacher_scores = scores[1, index, rows, lane]
                first_id = ((z * ring + index) * n_col + col) * per_device
                matched = jnp.where(offsets[rows] == first_id, 1.0, 0.0)
                weights = (
                    jnp.exp2(student_scores - row_tiles[0, rows])
                    + jnp.exp2(student_scores - col_lse[index, z, 0:1, :])
                    - jnp.exp2(teacher_scores - row_tiles[1, rows])
                    - jnp.exp2(teacher_scores - col_lse[index, z, 1:2, :])
                    - matched
                )
                parts.append(weights.astype(jnp.bfloat16))
            product = jnp.dot(
                jnp.concatenate(parts, axis=1),
                text_student(index),
                preferred_element_type=jnp.float32,
            )
            partial_grad[target] += product.reshape(2, per_device, width)
            return carry

        lax.fori_loop(0, ring, texts, 0)
        over[step] = mail.push(
            partial_grad.at[target, other], from_core.at[target], place.sibling()
        )

    def pass_over(step):
        target = place.along_y(step)
        mail.got(from_core.at[target], over[step])
        total = partial_grad[target, core] + from_core[target]
        if step:
            leaving[step - 1] = total.astype(jnp.bfloat16)
            across[step] = mail.push(
                leaving.at[step - 1], arriving.at[step - 1], place.to_y(step)
            )
        return total

    weigh(2)
    weigh(1)
    pass_over(2)
    weigh(3)
    pass_over(1)
    weigh(0)
    pass_over(3)
    embed_grad = pass_over(0)
    for step in (2, 1, 3):
        mail.got(arriving.at[step - 1], across[step])
        embed_grad = embed_grad + arriving[step - 1].astype(jnp.float32)
    embed_grad = logit_scale * embed_grad
    raw_student = raw_ref[...]
    scale = lax.rsqrt(jnp.sum(raw_student * raw_student, axis=1, keepdims=True) + norm_eps)
    student_unit = raw_student * scale
    inner_term = jnp.sum(student_unit * embed_grad, axis=1, keepdims=True)
    grad_embed = (embed_grad - student_unit * inner_term) * scale
    embed_out[...] = grad_embed
    rounded = grad_embed.astype(jnp.bfloat16)

    kinds, pieces, size = partial.shape[1], partial.shape[2], partial.shape[3]
    for side in range(2):
        for kind in range(kinds):
            start = (side * kinds + kind) * size
            product = lax.dot_general(
                si_ref[:, start : start + size],
                rounded,
                tn_dims,
                preferred_element_type=jnp.float32,
            )
            for lane in range(pieces):
                partial[side, kind, lane] = product[:, lane * size : (lane + 1) * size]
    ticket = mail.push(partial.at[other], from_sibling, place.sibling())
    mail.got(from_sibling, ticket)
    summed[...] = partial[core] + from_sibling[...]
    along = {
        "x": (place.x, place.along_x, place.to_x),
        "y": (place.y, place.along_y, place.to_y),
        "z": (place.z, place.along_z, place.to_z),
    }
    axes = ("yxz", "xzy", "zyx")

    def rows_of(position, count):
        return pl.ds(pl.multiple_of(position * count, 8), count)

    tickets = {}
    for kind in range(kinds):
        own, at, to = along[axes[kind][0]]
        for step in range(1, ring):
            tickets[kind, step] = mail.push(
                summed.at[kind, at(step)], first_in.at[kind, step - 1], to(step)
            )
    for kind in range(kinds):
        own, at, to = along[axes[kind][0]]
        total = summed[kind, own]
        for step in range(1, ring):
            mail.got(first_in.at[kind, step - 1], tickets[kind, step])
            total = total + first_in[kind, step - 1]
        second[kind] = total
        own, at, to = along[axes[kind][1]]
        for step in range(1, ring):
            tickets[kind, step] = mail.push(
                second.at[kind, rows_of(at(step), 32)], second_in.at[kind, step - 1], to(step)
            )
    for kind in range(kinds):
        own, at, to = along[axes[kind][1]]
        total = second[kind, rows_of(own, 32)]
        for step in range(1, ring):
            mail.got(second_in.at[kind, step - 1], tickets[kind, step])
            total = total + second_in[kind, step - 1]
        third[kind] = total
        own, at, to = along[axes[kind][2]]
        for step in range(1, ring):
            tickets[kind, step] = mail.push(
                third.at[kind, rows_of(at(step), 8)], third_in.at[kind, step - 1], to(step)
            )
    for kind in range(kinds):
        own, at, to = along[axes[kind][2]]
        total = third[kind, rows_of(own, 8)]
        for step in range(1, ring):
            mail.got(third_in.at[kind, step - 1], tickets[kind, step])
            total = total + third_in[kind, step - 1]
        fourth[kind] = total
        tickets[kind, 0] = mail.push(
            fourth.at[kind], fourth_in.at[kind], {"group": 1 - lax.axis_index("group")}
        )

    def piece(kind, level, step):
        own1, at1, to1 = along[axes[kind][0]]
        own2, at2, to2 = along[axes[kind][1]]
        own3, at3, to3 = along[axes[kind][2]]
        if level == 3:
            start = own2 * 32 + at3(step) * 8
            return proj_out.at[core, kind, own1, pl.ds(pl.multiple_of(start, 8), 8)]
        if level == 2:
            return proj_out.at[core, kind, own1, rows_of(at2(step), 32)]
        return proj_out.at[core, kind, at1(step)]

    def send_piece(kind, level):
        to = along[axes[kind][level - 1]][2]
        for step in range(1, ring):
            tickets[kind, step] = mail.push(
                piece(kind, level, 0), piece(kind, level, 0), to(step)
            )

    def land_piece(kind, level):
        for step in range(1, ring):
            mail.got(piece(kind, level, -step), tickets[kind, step])

    for kind in range(kinds):
        mail.got(fourth_in.at[kind], tickets[kind, 0])
        piece(kind, 3, 0)[...] = fourth[kind] + fourth_in[kind]
        send_piece(kind, 3)
    for level in (3, 2):
        for kind in range(kinds):
            land_piece(kind, level)
            send_piece(kind, level - 1)
    for kind in range(kinds):
        land_piece(kind, 1)
    ticket = mail.push(proj_out.at[core], proj_out.at[core], place.sibling())
    mail.got(proj_out.at[other], ticket)
    mail.finish()


def body(
    student_image,
    student_proj,
    student_text,
    teacher_image,
    teacher_proj,
    teacher_text,
    assignment,
    pair_ids,
):
    per_device, width = student_text.shape
    teacher_width = teacher_text.shape[1]
    student_width = student_image.shape[1]
    features, proj_width = teacher_proj.shape
    size = 128
    kinds = student_width // (2 * size)
    pieces = width // size
    bf16, f32, i32 = jnp.bfloat16, jnp.float32, jnp.int32
    tile = (8, per_device)
    chunk = ring * per_device
    images = n_col * per_device
    hbm = pl.BlockSpec(memory_space=pl.ANY)
    vmem = pl.BlockSpec(memory_space=pltpu.VMEM)
    copies = 216
    grad_embed, grad_proj = pl.pallas_call(
        step_kernel,
        out_shape=(
            jax.ShapeDtypeStruct((per_device, width), f32),
            jax.ShapeDtypeStruct((2, kinds, pieces, size, size), f32),
        ),
        in_specs=[hbm] * 8,
        out_specs=[vmem] * 2,
        scratch_shapes=[
            pltpu.VMEM(student_image.shape, bf16),
            pltpu.VMEM(student_proj.shape, bf16),
            pltpu.VMEM(student_text.shape, bf16),
            pltpu.VMEM((features, n_row * per_device), bf16),
            pltpu.VMEM(teacher_text.shape, bf16),
            pltpu.VMEM((ring, ring, per_device, teacher_width + width), bf16),
            pltpu.VMEM((n_col, per_device, width), bf16),
            pltpu.VMEM((n_col, per_device, teacher_width), bf16),
            pltpu.VMEM((n_col, 1, per_device), i32),
            pltpu.VMEM((per_device, width), f32),
            pltpu.VMEM((n_row, 1, per_device), i32),
            pltpu.VMEM((n_row, per_device, features), bf16),
            pltpu.VMEM((n_row, per_device, features), bf16),
            pltpu.VMEM((n_col, n_row, proj_width, features), bf16),
            pltpu.VMEM((teacher_width, per_device), f32),
            pltpu.VMEM((2, ring, images, chunk), f32),
            pltpu.VMEM((2, images, per_device), f32),
            pltpu.VMEM((2, images, per_device), f32),
            pltpu.VMEM((2, 8, chunk), f32),
            pltpu.VMEM((2, 8, chunk), f32),
            pltpu.VMEM((n_col,) + tile, f32),
            pltpu.VMEM((n_col,) + tile, f32),
            pltpu.VMEM((n_col,) + tile, f32),
            pltpu.VMEM((ring, ring) + tile, f32),
            pltpu.VMEM((ring, ring) + tile, f32),
            pltpu.VMEM((ring, ring) + tile, f32),
            pltpu.VMEM((2, images, per_device), f32),
            pltpu.VMEM((images, per_device), i32),
            pltpu.VMEM((ring, 2, per_device, width), f32),
            pltpu.VMEM((ring, per_device, width), f32),
            pltpu.VMEM((ring - 1, per_device, width), bf16),
            pltpu.VMEM((ring - 1, per_device, width), bf16),
            pltpu.VMEM((2, kinds, pieces, size, size), f32),
            pltpu.VMEM((kinds, pieces, size, size), f32),
            pltpu.VMEM((kinds, pieces, size, size), f32),
            pltpu.VMEM((kinds, ring - 1, size, size), f32),
            pltpu.VMEM((kinds, size, size), f32),
            pltpu.VMEM((kinds, ring - 1, size // 4, size), f32),
            pltpu.VMEM((kinds, size // 4, size), f32),
            pltpu.VMEM((kinds, ring - 1, 8, size), f32),
            pltpu.VMEM((kinds, 8, size), f32),
            pltpu.VMEM((kinds, 8, size), f32),
            pltpu.SemaphoreType.DMA((8,)),
            pltpu.SemaphoreType.DMA((copies,)),
            pltpu.SemaphoreType.DMA((copies,)),
        ],
        compiler_params=pltpu.CompilerParams(
            collective_id=0, has_side_effects=True, vmem_limit_bytes=60 * 1024 * 1024
        ),
    )(
        student_image,
        student_proj,
        student_text,
        teacher_image.T,
        teacher_proj.T,
        teacher_text,
        assignment,
        pair_ids,
    )
    return grad_embed, grad_proj.transpose(0, 1, 3, 2, 4).reshape(student_width, width)


def solution(mesh):
    placed = (
        P(("group", "row", "col"), None),
        P(),
        P(("group", "row", "col"), None),
        P(("group", "col"), "row"),
        P("row", "col"),
        P(("group", "row", "col"), None),
        P("group", ("row", "col")),
        P("group", ("row", "col")),
    )
    return jax.shard_map(
        body,
        mesh=mesh,
        in_specs=placed,
        out_specs=(P(("group", "row", "col"), None), P()),
        check_vma=False,
    )
```

time: 801 us -> 178 us (0.22)
  waiting for transfers between devices: 431 us -> 0 us
  blocking collectives: 286 us -> 0 us
  Pallas kernels: 0 us -> 173 us
  matrix products: 31 us -> 0 us
  other arithmetic: 15.9 us -> 0 us
  between operations: 16.3 us -> 0.65 us
    all_gather x11 -> x0, blocking collectives: 286 us -> none  [the longest x8 217 us: combined_all(): gathered = jax.tree.map(lambda a: lax.all_gather(a, axis), part)]
    psum x1 -> x0, waiting for transfers between devices: 259 us -> none  [body(): grad_proj = lax.psum(weight_partial, ('group', 'row', 'col'))]
    pallas_call x0 -> x1, Pallas kernels: none -> 173 us  [body(): pl.pallas_call(step_kernel, out_shape=(jax.ShapeDtypeStruct((per_device,...]
    reduce_scatter x2 -> x0, waiting for transfers between devices: 153 us -> none  [the longest x1 122 us: body(): lax.psum_scatter(jnp.dot(teacher_image, proj_rows, preferred_element_type...]
    dot_general x9 -> x0, matrix products: 31 us -> none  [the longest x4 13.2 us: tile_scores(): jnp.einsum('ik,jk->ij', images, texts, preferred_element_type=jnp.float32)]
    all_to_all x1 -> x0, waiting for transfers between devices: 19 us -> none  [body(): lax.all_to_all(outgoing, 'row', split_axis=0, concat_axis=0, tiled=True)]
    reduce_sum x9 -> x0, other arithmetic: 9.09 us -> none  [the longest x2 5.34 us: column_partial(): return (highest, jnp.sum(jnp.exp(values - highest[None, :]), axis=0))]
  transfers between devices with their start and end apart: 8 -> 0, of which waited for: 4 -> 0; matrix products, arithmetic and copies ran while one was open for 2% -> 0% of each run, Pallas kernels for 0% -> 0%
where the time goes in v1:
time: 178 us
  Pallas kernels  173 us (97%)
  local copies, waits for them, and re-layouts  4.39 us (2%)
    pallas_call x1, Pallas kernels, body(): pl.pallas_call(step_kernel, out_shape=(jax.ShapeDtypeStruct((per_device,...  173 us

profile of v1, /device:TPU:1, one launch (start us, length us, event | category | flops | bytes accessed | tf_op | source)
XLA Modules:
  0.0 177.9 jit_solution(12798385298300438402)
XLA Ops:
  0.6 172.9 %shard_map.95 = (f32[128,512]{1,0:T(8,128)}, f32[2,3,4,128,128]{4,3,2,1,0:T(8,128)}) custom-call(bf16[128,768]{1,0:T(8,128)(2,1)} %si_hbm.1, bf16[768,512]{1,0:T(8,128)(2,1)} %sp_hbm.1, bf16[128,512]{1,0:T(8,128)(2,1)} %st_hbm.1, bf16[104,2048]{1,0:T(8,128)(2,1)} %bitcast.11, bf16[160,104]{1,0:T(8,128)(2,1)} %bitcast.12, bf16[128,1280]{1,0:T(8,128)(2,1)} %tt_hbm.1, ...), custom_call_target="tpu_custom_call" | custom-call | tf_op jit(solution)/shard_map/pallas_call | solution.py:723
  173.5 2.4 %copy.10 = f32[2,3,128,4,128]{4,3,2,1,0:T(4,128)S(1)} copy(f32[2,3,128,4,128]{4,2,3,1,0:T(8,128)} %bitcast.10) | data formatting | bytes 3145728 | tf_op jit(solution)/shard_map/transpose | solution.py:791
  176.0 0.0 copy-start
  176.0 1.3 copy.13
  177.2 0.0 copy-done
  177.2 0.7 copy.15
Async XLA Ops:
  176.0 1.3 copy-start

commit v2 on v1

v2 whole, which is shorter than its diff:
```python
import math

import jax
import jax.numpy as jnp
from jax import lax
from jax.experimental import pallas as pl
from jax.experimental.pallas import tpu as pltpu
from jax.sharding import PartitionSpec as P

logit_scale = 100.0
score_scale = logit_scale * math.log2(math.e)
lowest = -1e30
norm_eps = 1e-06
MESH = pl.DeviceIdType.MESH
ring = 4
n_row = 16
n_col = 8
nt_dims = (((1,), (1,)), ((), ()))
tn_dims = (((0,), (0,)), ((), ()))


def unit_rows(values):
    return values * lax.rsqrt(jnp.sum(values * values, axis=1, keepdims=True) + norm_eps)


class Place:
    def __init__(self):
        self.row = lax.axis_index("row")
        self.col = lax.axis_index("col")
        self.z, self.x = self.row // ring, self.row % ring
        self.y, self.core = self.col // 2, self.col % 2
        self.slot = self.x * 2 + self.core

    def along_x(self, step):
        return (self.x + step + ring) % ring

    def along_y(self, step):
        return (self.y + step + ring) % ring

    def along_z(self, step):
        return (self.z + step + ring) % ring

    def to_x(self, step):
        return {"row": self.z * ring + self.along_x(step)}

    def to_z(self, step):
        return {"row": self.along_z(step) * ring + self.x}

    def to_y(self, step):
        return {"col": self.along_y(step) * 2 + self.core}

    def to_slot(self, step):
        slot = (self.slot + step) % n_col
        return {"row": self.z * ring + slot // 2, "col": self.y * 2 + slot % 2}

    def to_text(self, dy, dz):
        return {
            "row": self.along_z(dz) * ring + self.x,
            "col": self.along_y(dy) * 2 + self.core,
        }

    def across(self, step):
        return {
            "group": 1 - lax.axis_index("group"),
            "row": self.along_z(step) * ring + self.x,
        }

    def sibling(self):
        return {"col": self.y * 2 + 1 - self.core}


class Mail:
    def __init__(self, send_sem, recv_sem):
        self.send_sem, self.recv_sem = send_sem, recv_sem
        self.used = 0
        self.sent = {}

    def push(self, src, dst, device):
        index = self.used
        self.used += 1
        turn = index % self.send_sem.shape[0]
        if turn in self.sent:
            self.sent[turn].wait_send()
        copy = pltpu.make_async_remote_copy(
            src_ref=src,
            dst_ref=dst,
            send_sem=self.send_sem.at[turn],
            recv_sem=self.recv_sem.at[index],
            device_id=device,
            device_id_type=MESH,
        )
        copy.start()
        self.sent[turn] = copy
        return index, device

    def got(self, slot, ticket):
        index, device = ticket
        pltpu.make_async_remote_copy(
            src_ref=slot,
            dst_ref=slot,
            send_sem=self.send_sem.at[0],
            recv_sem=self.recv_sem.at[index],
            device_id=device,
            device_id_type=MESH,
        ).wait_recv()

    def finish(self):
        for copy in self.sent.values():
            copy.wait_send()


def all_peers(place):
    return (
        [{"row": (place.row + step) % n_row} for step in range(1, n_row)]
        + [place.to_text(dy, dz) for dy in range(1, ring) for dz in range(ring)]
        + [
            {
                "row": place.z * ring + place.along_x(step),
                "col": place.y * 2 + 1 - place.core,
            }
            for step in range(ring)
        ]
        + [place.across(step) for step in range(ring)]
    )


class AlongX:
    def __init__(self, mail, place, ref, first=0, count=None):
        self.mail, self.place, self.ref = mail, place, ref
        self.first, self.count = first, count or ref.shape[1]
        self.half = self.count // 2

    def whole(self, index):
        return self.ref.at[index, pl.ds(self.first, self.count)]

    def block(self, step, core):
        return self.place.along_x(step) * 2 + core

    def lower(self, index):
        return self.ref.at[index, pl.ds(self.first, self.half)]

    def upper(self, index):
        return self.ref.at[index, pl.ds(self.first + self.half, self.half)]

    def start(self):
        place, mail = self.place, self.mail
        own = self.whole(place.slot)
        self.up = mail.push(own, own, place.to_x(1))
        self.down = mail.push(own, own, place.to_x(-1))
        self.over = [mail.push(own, own, place.sibling())]

    def forward(self):
        place, mail = self.place, self.mail
        below = self.block(-1, place.core)
        mail.got(self.whole(below), self.up)
        self.up_half = mail.push(self.lower(below), self.lower(below), place.to_x(1))
        self.over.append(mail.push(self.whole(below), self.whole(below), place.sibling()))
        above = self.block(1, place.core)
        mail.got(self.whole(above), self.down)
        self.down_half = mail.push(self.upper(above), self.upper(above), place.to_x(-1))
        self.over.append(mail.push(self.whole(above), self.whole(above), place.sibling()))

    def last(self):
        place, mail = self.place, self.mail
        far = self.block(2, place.core)
        mail.got(self.lower(far), self.up_half)
        self.over.append(mail.push(self.lower(far), self.lower(far), place.sibling()))
        mail.got(self.upper(far), self.down_half)
        self.over.append(mail.push(self.upper(far), self.upper(far), place.sibling()))

    def end(self):
        place, mail = self.place, self.mail
        other = 1 - place.core
        mail.got(self.whole(self.block(0, other)), self.over[0])
        mail.got(self.whole(self.block(-1, other)), self.over[1])
        mail.got(self.whole(self.block(1, other)), self.over[2])
        far = self.block(2, other)
        mail.got(self.lower(far), self.over[3])
        mail.got(self.upper(far), self.over[4])


def step_kernel(
    si_hbm,
    sp_hbm,
    st_hbm,
    ti_hbm,
    pt_hbm,
    tt_hbm,
    order_hbm,
    pair_hbm,
    embed_out,
    proj_out,
    si_ref,
    sp_ref,
    st_ref,
    ti_ref,
    tt_ref,
    text,
    img_s,
    img_t,
    pairs,
    raw_ref,
    orders,
    feat_out,
    feat_in,
    proj,
    embed,
    scores,
    row_high,
    row_total,
    col_high,
    col_total,
    row_stats,
    row_landed,
    row_lse,
    col_stats,
    col_landed,
    col_lse,
    row_tiles,
    offsets,
    partial_grad,
    from_core,
    leaving,
    arriving,
    si_sibling,
    grads,
    grads_sibling,
    summed,
    first_out,
    first_in,
    second,
    second_out,
    second_in,
    third,
    third_in,
    group_sums,
    gathered,
    load_sem,
    send_sem,
    recv_sem,
):
    place = Place()
    mail = Mail(send_sem, recv_sem)
    row, col, core, slot = place.row, place.col, place.core, place.slot
    other = 1 - core
    per_device, width = st_ref.shape
    teacher_width = tt_ref.shape[1]
    half = per_device // 2
    share = si_ref.shape[1] // 2

    loads = []
    for source, target in (
        (order_hbm, orders.at[row]),
        (pt_hbm, proj.at[slot, place.y * ring + place.z]),
        (pair_hbm, pairs.at[slot]),
        (st_hbm, st_ref),
        (tt_hbm, tt_ref),
        (si_hbm, si_ref),
        (sp_hbm, sp_ref),
        (ti_hbm, ti_ref),
    ):
        copy = pltpu.make_async_copy(source, target, load_sem.at[len(loads)])
        copy.start()
        loads.append(copy)
    barrier = pltpu.get_barrier_semaphore()
    peers = all_peers(place)
    for device in peers:
        pl.semaphore_signal(barrier, inc=1, device_id=device, device_id_type=MESH)
    for copy in loads[:5]:
        copy.wait()
    own_y, own_z = place.y, place.z
    text[own_z, own_y, :, :teacher_width] = unit_rows(tt_ref[...].astype(jnp.float32)).astype(
        jnp.bfloat16
    )
    text[own_z, own_y, :, teacher_width:] = unit_rows(st_ref[...].astype(jnp.float32)).astype(
        jnp.bfloat16
    )
    pl.semaphore_wait(barrier, len(peers))

    own_proj = proj.at[slot, place.y * ring + place.z]
    proj_z = [mail.push(own_proj, own_proj, place.to_z(step)) for step in (1, 3, 2)]

    def block(dy, dz, part):
        return text.at[place.along_z(dz), place.along_y(dy), pl.ds(part * half, half)]

    z_up, z_down, y_up, y_down, y_on = {}, {}, {}, {}, {}

    def start_z(part):
        z_up[part] = mail.push(block(0, 0, part), block(0, 0, part), place.to_z(1))
        z_down[part] = mail.push(block(0, 0, part), block(0, 0, part), place.to_z(-1))

    def start_y(dz, part):
        y_up[dz, part] = mail.push(block(0, dz, part), block(0, dz, part), place.to_y(1))
        y_down[dz, part] = mail.push(block(0, dz, part), block(0, dz, part), place.to_y(-1))

    def forward_y(dz):
        mail.got(block(-1, dz, 0), y_up[dz, 0])
        y_on[dz, 0] = mail.push(block(-1, dz, 0), block(-1, dz, 0), place.to_y(1))
        mail.got(block(1, dz, 1), y_down[dz, 1])
        y_on[dz, 1] = mail.push(block(1, dz, 1), block(1, dz, 1), place.to_y(-1))

    start_z(0)
    start_y(0, 0)
    own_order = orders.at[row]
    order_mail = [
        mail.push(own_order, own_order, {"row": (row + step) % n_row}) for step in range(1, n_row)
    ]
    loads[5].wait()
    loads[6].wait()
    si_mail = mail.push(
        si_ref.at[:, pl.ds(pl.multiple_of(other * share, share), share)],
        si_sibling,
        place.sibling(),
    )
    raw_student = jnp.dot(si_ref[...], sp_ref[...], preferred_element_type=jnp.float32)
    raw_ref[...] = raw_student
    img_s[slot] = unit_rows(raw_student).astype(jnp.bfloat16)
    for step, ticket in zip((1, 3, 2), proj_z):
        mail.got(proj.at[slot, place.y * ring + place.along_z(-step)], ticket)

    def proj_rows(step, start=0, count=ring):
        return proj.at[slot, pl.ds(place.along_y(step) * ring + start, count)]

    def proj_spread(step):
        spread = AlongX(mail, place, proj, place.along_y(step) * ring, ring)
        spread.start()
        return spread

    proj_up = mail.push(proj_rows(0), proj_rows(0), place.to_y(1))
    proj_down = mail.push(proj_rows(0), proj_rows(0), place.to_y(-1))
    spreads = [proj_spread(0)]
    start_z(1)
    start_y(0, 1)
    student = AlongX(mail, place, img_s)
    student.start()
    own_pairs = pairs.at[slot]
    pair_mail = [mail.push(own_pairs, own_pairs, place.to_slot(step)) for step in range(1, n_col)]

    image_rows = 2 * per_device
    chunk = ring * per_device
    col_mail = {}

    def end_y(dz):
        mail.got(block(-1, dz, 1), y_up[dz, 1])
        mail.got(block(1, dz, 0), y_down[dz, 0])
        mail.got(block(2, dz, 0), y_on[dz, 0])
        mail.got(block(2, dz, 1), y_on[dz, 1])

    def prepare():
        end_y(0)
        for step in range(1, n_col):
            mail.got(pairs.at[(slot + n_col - step) % n_col], pair_mail[step - 1])
        lane_ids = lax.broadcasted_iota(jnp.int32, (per_device, per_device), 1)
        for source in range(n_col):
            wide = jnp.broadcast_to(pairs[source].astype(jnp.float32), (per_device, per_device)).T
            offsets[source * per_device : (source + 1) * per_device] = (
                wide.astype(jnp.int32) - lane_ids
            )
        row_high[...] = jnp.full(row_high.shape, lowest, jnp.float32)
        row_total[...] = jnp.zeros(row_total.shape, jnp.float32)
        col_stats[...] = jnp.zeros(col_stats.shape, jnp.float32)

    def text_student(index):
        return text[index, :, :, teacher_width:].reshape(chunk, width)

    def text_teacher(index):
        return text[index, :, :, :teacher_width].reshape(chunk, teacher_width)

    def process(kind, dz):
        index = place.along_z(dz)
        col_high[...] = jnp.full(col_high.shape, lowest, jnp.float32)
        col_total[...] = jnp.zeros(col_total.shape, jnp.float32)

        def images(step, carry):
            rows = pl.ds(pl.multiple_of(step * image_rows, image_rows), image_rows)
            if kind == 0:
                left = img_s[pl.ds(2 * step, 2)].reshape(image_rows, width)
                right = text_student(index)
            else:
                left = img_t[pl.ds(2 * step, 2)].reshape(image_rows, teacher_width)
                right = text_teacher(index)
            values = score_scale * lax.dot_general(
                left, right, nt_dims, preferred_element_type=jnp.float32
            )
            scores[kind, index, rows] = values
            tiles = [values[:, start : start + per_device] for start in range(0, chunk, per_device)]
            before = row_high[kind, rows]
            high = before
            for tile in tiles:
                high = jnp.maximum(high, tile)
            total = row_total[kind, rows] * jnp.exp2(before - high)
            for tile in tiles:
                total = total + jnp.exp2(tile - high)
            row_high[kind, rows] = high
            row_total[kind, rows] = total
            stacked = values.reshape(image_rows // 8, 8, chunk)
            before = col_high[...]
            high = jnp.maximum(before, jnp.max(stacked, axis=0))
            total = col_total[...] * jnp.exp2(before - high)
            col_total[...] = total + jnp.sum(jnp.exp2(stacked - high[None]), axis=0)
            col_high[...] = high
            return carry

        lax.fori_loop(0, ring, images, 0)
        high = jnp.max(col_high[...], axis=0, keepdims=True)
        total = jnp.sum(col_total[...] * jnp.exp2(col_high[...] - high), axis=0, keepdims=True)
        for y in range(ring):
            lane = slice(y * per_device, (y + 1) * per_device)
            col_stats[index, y, 2 * kind : 2 * kind + 1] = high[:, lane]
            col_stats[index, y, 2 * kind + 1 : 2 * kind + 2] = total[:, lane]
        if kind == 1:
            for dy in range(ring):
                y = place.along_y(dy)
                if dy or dz:
                    col_mail[dy, dz % ring] = mail.push(
                        col_stats.at[index, y],
                        col_landed.at[own_y, own_z],
                        place.to_text(dy, dz),
                    )
                else:
                    col_landed[own_y, own_z] = col_stats[index, y]

    loads[7].wait()
    for step in range(1, n_row):
        mail.got(orders.at[(row + n_row - step) % n_row], order_mail[step - 1])
    lanes = lax.broadcasted_iota(jnp.int32, (per_device, 2 * per_device), 1).astype(jnp.float32)

    def pick(target, carry):
        wanted = (orders[target] - col * (n_row * per_device)).astype(jnp.float32)
        wanted = jnp.broadcast_to(wanted, (per_device, per_device)).T
        wanted = jnp.concatenate([wanted, wanted], axis=1)
        total = jnp.zeros((per_device, ti_ref.shape[0]), jnp.float32)
        for start in range(0, n_row * per_device, 2 * per_device):
            chosen = jnp.where(wanted == lanes + float(start), 1.0, 0.0).astype(jnp.bfloat16)
            total += lax.dot_general(
                chosen,
                ti_ref[:, start : start + 2 * per_device],
                nt_dims,
                preferred_element_type=jnp.float32,
            )
        feat_out[target] = total.astype(jnp.bfloat16)
        return carry

    half_rows = ring // 2
    lower, upper = (0, half_rows), (half_rows, half_rows)
    lax.fori_loop(0, n_row // 2, pick, 0)
    mail.got(proj_rows(-1), proj_up)
    proj_up = mail.push(proj_rows(-1, *lower), proj_rows(-1, *lower), place.to_y(1))
    spreads.append(proj_spread(-1))
    mail.got(proj_rows(1), proj_down)
    proj_down = mail.push(proj_rows(1, *upper), proj_rows(1, *upper), place.to_y(-1))
    spreads.append(proj_spread(1))
    spreads[0].forward()
    lax.fori_loop(n_row // 2, n_row, pick, 0)
    feat_mail = []
    for step in range(1, n_row):
        target = (row + step) % n_row
        feat_mail.append(mail.push(feat_out.at[target], feat_in.at[row], {"row": target}))
    feat_in[row] = feat_out[row]
    mail.got(proj_rows(2, *lower), proj_up)
    mail.got(proj_rows(2, *upper), proj_down)
    spreads.append(proj_spread(2))

    mail.got(block(0, -1, 0), z_up[0])
    z_up_on = mail.push(block(0, -1, 0), block(0, -1, 0), place.to_z(1))
    start_y(-1, 0)
    mail.got(block(0, 1, 0), z_down[0])
    start_y(1, 0)
    forward_y(0)
    spreads[0].last()
    spreads[1].forward()
    spreads[2].forward()
    mail.got(block(0, 1, 1), z_down[1])
    z_down_on = mail.push(block(0, 1, 1), block(0, 1, 1), place.to_z(-1))
    start_y(1, 1)
    mail.got(block(0, -1, 1), z_up[1])
    start_y(-1, 1)
    spreads[1].last()
    spreads[2].last()
    spreads[3].forward()
    student.forward()
    spreads[3].last()
    student.last()
    student.end()
    prepare()
    process(0, 0)
    mail.got(block(0, 2, 0), z_up_on)
    start_y(2, 0)
    mail.got(block(0, 2, 1), z_down_on)
    start_y(2, 1)
    for spread in spreads:
        spread.end()
    for step in range(1, n_row):
        mail.got(feat_in.at[(row + n_row - step) % n_row], feat_mail[step - 1])
    proj_width = proj.shape[2]

    def project(source, carry):
        total = jnp.zeros((proj_width, per_device), jnp.float32)
        for features in range(n_row):
            z, x = features // ring, features % ring
            total += lax.dot_general(
                proj[x * 2 + source % 2, source // 2 * ring + z],
                feat_in[features],
                nt_dims,
                preferred_element_type=jnp.float32,
            )
        embed[pl.ds(pl.multiple_of(source * proj_width, 8), proj_width), :] = total
        return carry

    lax.fori_loop(0, n_col, project, 0)
    raw_teacher = embed[...]
    scale = lax.rsqrt(jnp.sum(raw_teacher * raw_teacher, axis=0, keepdims=True) + norm_eps)
    img_t[slot] = (raw_teacher * scale).T.astype(jnp.bfloat16)
    teacher = AlongX(mail, place, img_t)
    teacher.start()
    forward_y(-1)
    teacher.forward()
    forward_y(1)
    end_y(-1)
    process(0, -1)
    teacher.last()
    end_y(1)
    process(0, 1)
    forward_y(2)
    teacher.end()
    process(1, 0)
    process(1, -1)
    process(1, 1)
    end_y(2)
    process(0, 2)
    process(1, 2)

    for source in range(n_col):
        rows = slice(source * per_device, (source + 1) * per_device)
        found = []
        for kind in range(2):
            high_all = row_high[kind, rows].T
            high = jnp.max(high_all, axis=0, keepdims=True)
            total = jnp.sum(
                row_total[kind, rows].T * jnp.exp2(high_all - high), axis=0, keepdims=True
            )
            found += [high, total]
        row_stats[source] = jnp.concatenate(
            found + [jnp.zeros((4, per_device), jnp.float32)], axis=0
        )
    row_mail = [
        mail.push(
            row_stats.at[(slot + step) % n_col], row_landed.at[slot], place.to_slot(step)
        )
        for step in range(1, n_col)
    ]
    row_landed[slot] = row_stats[slot]

    def merge(parts):
        found = []
        for kind in range(2):
            high = jnp.max(parts[:, 2 * kind], axis=0, keepdims=True)
            total = jnp.sum(
                parts[:, 2 * kind + 1] * jnp.exp2(parts[:, 2 * kind] - high),
                axis=0,
                keepdims=True,
            )
            found.append(high + jnp.log2(total) + float(kind))
        return jnp.concatenate(found + [jnp.zeros((6, per_device), jnp.float32)], axis=0)

    pairs_of_steps = [(dy, dz) for dy in range(ring) for dz in range(ring) if dy or dz]
    for dy, dz in pairs_of_steps:
        mail.got(col_landed.at[place.along_y(-dy), place.along_z(-dz)], col_mail[dy, dz])
    col_lse[own_y, own_z] = merge(col_landed[...].reshape(n_row, 8, per_device))
    own_lse = col_lse.at[own_y, own_z]
    col_back = {
        (dy, dz): mail.push(own_lse, own_lse, place.to_text(dy, dz)) for dy, dz in pairs_of_steps
    }
    for step in range(1, n_col):
        mail.got(row_landed.at[(slot + n_col - step) % n_col], row_mail[step - 1])
    row_lse[slot] = merge(row_landed[...])
    row_back = [
        mail.push(row_lse.at[slot], row_lse.at[slot], place.to_slot(step))
        for step in range(1, n_col)
    ]
    for step in range(1, n_col):
        mail.got(row_lse.at[(slot + n_col - step) % n_col], row_back[step - 1])
    for source in range(n_col):
        rows = slice(source * per_device, (source + 1) * per_device)
        for kind in range(2):
            wide = row_lse[source, kind : kind + 1, :]
            row_tiles[kind, rows] = jnp.broadcast_to(wide, (per_device, per_device)).T
    for dy, dz in pairs_of_steps:
        mail.got(col_lse.at[place.along_y(-dy), place.along_z(-dz)], col_back[dy, dz])

    over = {}
    across = {}

    def weigh(step):
        target = place.along_x(step)
        rows = pl.ds(pl.multiple_of(target * image_rows, image_rows), image_rows)
        partial_grad[target] = jnp.zeros(partial_grad.shape[1:], jnp.float32)

        def texts(index, carry):
            parts = []
            for y in range(ring):
                lane = slice(y * per_device, (y + 1) * per_device)
                student_scores = scores[0, index, rows, lane]
                teacher_scores = scores[1, index, rows, lane]
                first_id = ((index * ring + place.x) * n_col + y * 2 + core) * per_device
                matched = jnp.where(offsets[rows] == first_id, 1.0, 0.0)
                weights = (
                    jnp.exp2(student_scores - row_tiles[0, rows])
                    + jnp.exp2(student_scores - col_lse[y, index, 0:1, :])
                    - jnp.exp2(teacher_scores - row_tiles[1, rows])
                    - jnp.exp2(teacher_scores - col_lse[y, index, 1:2, :])
                    - matched
                )
                parts.append(weights.astype(jnp.bfloat16))
            product = jnp.dot(
                jnp.concatenate(parts, axis=1),
                text_student(index),
                preferred_element_type=jnp.float32,
            )
            partial_grad[target] += product.reshape(2, per_device, width)
            return carry

        lax.fori_loop(0, ring, texts, 0)
        over[step] = mail.push(
            partial_grad.at[target, other], from_core.at[target], place.sibling()
        )

    def pass_over(step):
        target = place.along_x(step)
        mail.got(from_core.at[target], over[step])
        total = partial_grad[target, core] + from_core[target]
        if step:
            leaving[step - 1] = total.astype(jnp.bfloat16)
            across[step] = mail.push(
                leaving.at[step - 1], arriving.at[step - 1], place.to_x(step)
            )
        return total

    weigh(2)
    weigh(1)
    pass_over(2)
    weigh(3)
    pass_over(1)
    weigh(0)
    pass_over(3)
    embed_grad = pass_over(0)
    for step in (2, 1, 3):
        mail.got(arriving.at[step - 1], across[step])
        embed_grad = embed_grad + arriving[step - 1].astype(jnp.float32)
    embed_grad = logit_scale * embed_grad
    raw_student = raw_ref[...]
    scale = lax.rsqrt(jnp.sum(raw_student * raw_student, axis=1, keepdims=True) + norm_eps)
    student_unit = raw_student * scale
    inner_term = jnp.sum(student_unit * embed_grad, axis=1, keepdims=True)
    grad_embed = (embed_grad - student_unit * inner_term) * scale
    embed_out[...] = grad_embed
    grads[...] = grad_embed.astype(jnp.bfloat16)
    ticket = mail.push(grads, grads_sibling, place.sibling())

    pieces, kinds, size = summed.shape[:3]
    for kind in range(kinds):
        start = pl.multiple_of(core * share + kind * size, size)
        product = lax.dot_general(
            si_ref[:, pl.ds(start, size)],
            grads[...],
            tn_dims,
            preferred_element_type=jnp.float32,
        )
        for lane in range(pieces):
            summed[lane, kind] = product[:, lane * size : (lane + 1) * size]
    mail.got(si_sibling, si_mail)
    mail.got(grads_sibling, ticket)
    for kind in range(kinds):
        product = lax.dot_general(
            si_sibling[:, kind * size : (kind + 1) * size],
            grads_sibling[...],
            tn_dims,
            preferred_element_type=jnp.float32,
        )
        for lane in range(pieces):
            total = summed[lane, kind] + product[:, lane * size : (lane + 1) * size]
            summed[lane, kind] = total
            first_out[lane, kind] = total.astype(jnp.bfloat16)

    along_x = (place.x, place.along_x, place.to_x)
    along_y = (place.y, place.along_y, place.to_y)
    families = ((pl.ds(0, 2), along_y, along_x), (pl.ds(2, 1), along_x, along_y))
    quarter, tile = size // ring, size // n_row
    steps = (2, 1, 3)

    def rows_of(position, count):
        return pl.ds(pl.multiple_of(position * count, count), count)

    tickets = {}
    for index, (chosen, (own, at, to), _) in enumerate(families):
        for step in steps:
            tickets[index, step] = mail.push(
                first_out.at[at(step), chosen], first_in.at[step - 1, chosen], to(step)
            )
    for index, (chosen, (own, at, to), (own_next, at_next, to_next)) in enumerate(families):
        total = summed[own, chosen]
        for step in steps:
            mail.got(first_in.at[step - 1, chosen], tickets[index, step])
            total = total + first_in[step - 1, chosen].astype(jnp.float32)
        second[chosen] = total
        second_out[chosen] = total.astype(jnp.bfloat16)
        for step in steps:
            tickets[index, step] = mail.push(
                second_out.at[chosen, rows_of(at_next(step), quarter)],
                second_in.at[step - 1, chosen],
                to_next(step),
            )
    for index, (chosen, _, (own, at, to)) in enumerate(families):
        total = second[chosen, rows_of(own, quarter)]
        for step in steps:
            mail.got(second_in.at[step - 1, chosen], tickets[index, step])
            total = total + second_in[step - 1, chosen].astype(jnp.float32)
        third[chosen] = total
    for step in steps:
        tickets[step] = mail.push(
            third.at[:, rows_of(place.along_z(step), tile)], third_in.at[step - 1], place.to_z(step)
        )
    total = third[:, rows_of(place.z, tile)]
    for step in steps:
        mail.got(third_in.at[step - 1], tickets[step])
        total = total + third_in[step - 1]
    group = lax.axis_index("group")

    def group_tile(side, step):
        return group_sums.at[side, :, rows_of(place.along_z(step), tile)]

    group_tile(group, 0)[...] = total
    own_tile = group_tile(group, 0)
    for step in steps:
        tickets[0, step] = mail.push(own_tile, own_tile, place.to_z(step))
    for step in range(ring):
        tickets[1, step] = mail.push(own_tile, own_tile, place.across(step))
    for step in steps:
        mail.got(group_tile(group, -step), tickets[0, step])
    for step in range(ring):
        mail.got(group_tile(1 - group, -step), tickets[1, step])
    total = (group_sums[0] + group_sums[1]).astype(jnp.bfloat16)

    for index, (chosen, (own1, at1, to1), (own2, at2, to2)) in enumerate(families):
        mine = gathered.at[core, own1, chosen, rows_of(own2, quarter)]
        mine[...] = total[chosen.start : chosen.start + chosen.size]
        for step in steps:
            tickets[index, step] = mail.push(mine, mine, to2(step))
    back = {}
    for index, (chosen, (own1, at1, to1), (own2, at2, to2)) in enumerate(families):
        for step in steps:
            mail.got(
                gathered.at[core, own1, chosen, rows_of(at2(-step), quarter)],
                tickets[index, step],
            )
        mine = gathered.at[core, own1, chosen]
        for step in steps:
            tickets[index, step] = mail.push(mine, mine, to1(step))
        back[index, 0] = mail.push(mine, mine, place.sibling())
    for step in (1, 3, 2):
        for index, (chosen, (own1, at1, to1), _) in enumerate(families):
            theirs = gathered.at[core, at1(-step), chosen]
            mail.got(theirs, tickets[index, step])
            back[index, step] = mail.push(theirs, theirs, place.sibling())

    def write(side):
        for kind in range(kinds):
            rows = pl.ds(pl.multiple_of((side * kinds + kind) * size, size), size)
            for lane in range(pieces):
                proj_out[rows, lane * size : (lane + 1) * size] = gathered[
                    side, lane, kind
                ].astype(jnp.float32)

    write(core)
    for step in (0, 1, 3, 2):
        for index, (chosen, (own1, at1, to1), _) in enumerate(families):
            mail.got(gathered.at[other, at1(-step), chosen], back[index, step])
    write(other)
    mail.finish()


def body(
    student_image,
    student_proj,
    student_text,
    teacher_image,
    teacher_proj,
    teacher_text,
    assignment,
    pair_ids,
):
    per_device, width = student_text.shape
    teacher_width = teacher_text.shape[1]
    student_width = student_image.shape[1]
    features, proj_width = teacher_proj.shape
    size = 128
    kinds = student_width // (2 * size)
    pieces = width // size
    bf16, f32, i32 = jnp.bfloat16, jnp.float32, jnp.int32
    tile = (8, per_device)
    chunk = ring * per_device
    images = n_col * per_device
    hbm = pl.BlockSpec(memory_space=pl.ANY)
    vmem = pl.BlockSpec(memory_space=pltpu.VMEM)
    copies = 230
    grad_embed, grad_proj = pl.pallas_call(
        step_kernel,
        out_shape=(
            jax.ShapeDtypeStruct((per_device, width), f32),
            jax.ShapeDtypeStruct((student_width, width), f32),
        ),
        in_specs=[hbm] * 8,
        out_specs=[vmem] * 2,
        scratch_shapes=[
            pltpu.VMEM(student_image.shape, bf16),
            pltpu.VMEM(student_proj.shape, bf16),
            pltpu.VMEM(student_text.shape, bf16),
            pltpu.VMEM((features, n_row * per_device), bf16),
            pltpu.VMEM(teacher_text.shape, bf16),
            pltpu.VMEM((ring, ring, per_device, teacher_width + width), bf16),
            pltpu.VMEM((n_col, per_device, width), bf16),
            pltpu.VMEM((n_col, per_device, teacher_width), bf16),
            pltpu.VMEM((n_col, 1, per_device), i32),
            pltpu.VMEM((per_device, width), f32),
            pltpu.VMEM((n_row, 1, per_device), i32),
            pltpu.VMEM((n_row, per_device, features), bf16),
            pltpu.VMEM((n_row, per_device, features), bf16),
            pltpu.VMEM((n_col, n_row, proj_width, features), bf16),
            pltpu.VMEM((teacher_width, per_device), f32),
            pltpu.VMEM((2, ring, images, chunk), f32),
            pltpu.VMEM((2, images, per_device), f32),
            pltpu.VMEM((2, images, per_device), f32),
            pltpu.VMEM((8, chunk), f32),
            pltpu.VMEM((8, chunk), f32),
            pltpu.VMEM((n_col,) + tile, f32),
            pltpu.VMEM((n_col,) + tile, f32),
            pltpu.VMEM((n_col,) + tile, f32),
            pltpu.VMEM((ring, ring) + tile, f32),
            pltpu.VMEM((ring, ring) + tile, f32),
            pltpu.VMEM((ring, ring) + tile, f32),
            pltpu.VMEM((2, images, per_device), f32),
            pltpu.VMEM((images, per_device), i32),
            pltpu.VMEM((ring, 2, per_device, width), f32),
            pltpu.VMEM((ring, per_device, width), f32),
            pltpu.VMEM((ring - 1, per_device, width), bf16),
            pltpu.VMEM((ring - 1, per_device, width), bf16),
            pltpu.VMEM((per_device, student_width // 2), bf16),
            pltpu.VMEM((per_device, width), bf16),
            pltpu.VMEM((per_device, width), bf16),
            pltpu.VMEM((pieces, kinds, size, size), f32),
            pltpu.VMEM((pieces, kinds, size, size), bf16),
            pltpu.VMEM((ring - 1, kinds, size, size), bf16),
            pltpu.VMEM((kinds, size, size), f32),
            pltpu.VMEM((kinds, size, size), bf16),
            pltpu.VMEM((ring - 1, kinds, size // 4, size), bf16),
            pltpu.VMEM((kinds, size // 4, size), f32),
            pltpu.VMEM((ring - 1, kinds, 8, size), f32),
            pltpu.VMEM((2, kinds, size // 4, size), f32),
            pltpu.VMEM((2, pieces, kinds, size, size), bf16),
            pltpu.SemaphoreType.DMA((8,)),
            pltpu.SemaphoreType.DMA((96,)),
            pltpu.SemaphoreType.DMA((copies,)),
        ],
        compiler_params=pltpu.CompilerParams(
            collective_id=0, has_side_effects=True, vmem_limit_bytes=60 * 1024 * 1024
        ),
    )(
        student_image,
        student_proj,
        student_text,
        teacher_image.T,
        teacher_proj.T,
        teacher_text,
        assignment,
        pair_ids,
    )
    return grad_embed, grad_proj


def solution(mesh):
    placed = (
        P(("group", "row", "col"), None),
        P(),
        P(("group", "row", "col"), None),
        P(("group", "col"), "row"),
        P("row", "col"),
        P(("group", "row", "col"), None),
        P("group", ("row", "col")),
        P("group", ("row", "col")),
    )
    return jax.shard_map(
        body,
        mesh=mesh,
        in_specs=placed,
        out_specs=(P(("group", "row", "col"), None), P()),
        check_vma=False,
    )
```

time: 178 us -> 168 us (0.944)
  Pallas kernels: 173 us -> 163 us
    pallas_call x1, Pallas kernels: 173 us -> 163 us  [body(): pl.pallas_call(step_kernel, out_shape=(jax.ShapeDtypeStruct((per_device,...]
    transpose x1 -> x0, local copies, waits for them, and re-layouts: 2.42 us -> none  [body(): grad_proj.transpose(0, 1, 3, 2, 4).reshape(student_width, width)]
    unnamed x4 -> x2, local copies, waits for them, and re-layouts: 1.97 us -> 4.34 us
where the time goes in v2:
time: 168 us
  Pallas kernels  163 us (97%)
  local copies, waits for them, and re-layouts  4.34 us (3%)
    pallas_call x1, Pallas kernels, body(): pl.pallas_call(step_kernel, out_shape=(jax.ShapeDtypeStruct((per_device,...  163 us
    unnamed x2, local copies, waits for them, and re-layouts  4.34 us

profile of v2, /device:TPU:1, one launch (start us, length us, event | category | flops | bytes accessed | tf_op | source)
XLA Modules:
  0.0 167.7 jit_solution(12277583038891772570)
XLA Ops:
  0.6 162.8 %shard_map.95 = (f32[128,512]{1,0:T(8,128)}, f32[768,512]{1,0:T(8,128)}) custom-call(bf16[128,768]{1,0:T(8,128)(2,1)} %si_hbm.1, bf16[768,512]{1,0:T(8,128)(2,1)} %sp_hbm.1, bf16[128,512]{1,0:T(8,128)(2,1)} %st_hbm.1, bf16[104,2048]{1,0:T(8,128)(2,1)} %bitcast.2, bf16[160,104]{1,0:T(8,128)(2,1)} %bitcast.3, bf16[128,1280]{1,0:T(8,128)(2,1)} %tt_hbm.1, ...), custom_call_target="tpu_custom_call" | custom-call | tf_op jit(solution)/shard_map/pallas_call | solution.py:806
  163.4 1.7 copy.12
  165.1 2.7 %copy.13 = f32[768,512]{1,0:T(8,128)} copy(f32[768,512]{1,0:T(8,128)} %get-tuple-element.5) | data formatting | bytes 3145728

commit v3 on v2

--- a/solution.py
+++ b/solution.py
@@ -189,7 +189,7 @@
     order_hbm,
     pair_hbm,
     embed_out,
-    proj_out,
+    gathered,
     si_ref,
     sp_ref,
     st_ref,
@@ -234,7 +234,6 @@
     third,
     third_in,
     group_sums,
-    gathered,
     load_sem,
     send_sem,
     recv_sem,
@@ -245,9 +244,13 @@
     other = 1 - core
     per_device, width = st_ref.shape
     teacher_width = tt_ref.shape[1]
-    half = per_device // 2
+    first_part, second_part = 3 * per_device // 8, per_device // 2
     share = si_ref.shape[1] // 2
 
+    barrier = pltpu.get_barrier_semaphore()
+    peers = all_peers(place)
+    for device in peers:
+        pl.semaphore_signal(barrier, inc=1, device_id=device, device_id_type=MESH)
     loads = []
     for source, target in (
         (order_hbm, orders.at[row]),
@@ -262,10 +265,6 @@
         copy = pltpu.make_async_copy(source, target, load_sem.at[len(loads)])
         copy.start()
         loads.append(copy)
-    barrier = pltpu.get_barrier_semaphore()
-    peers = all_peers(place)
-    for device in peers:
-        pl.semaphore_signal(barrier, inc=1, device_id=device, device_id_type=MESH)
     for copy in loads[:5]:
         copy.wait()
     own_y, own_z = place.y, place.z
@@ -281,7 +280,15 @@
     proj_z = [mail.push(own_proj, own_proj, place.to_z(step)) for step in (1, 3, 2)]
 
     def block(dy, dz, part):
-        return text.at[place.along_z(dz), place.along_y(dy), pl.ds(part * half, half)]
+        start, count = ((0, first_part), (first_part, second_part))[part]
+        return text.at[place.along_z(dz), place.along_y(dy), pl.ds(start, count)]
+
+    def last_rows(dz, first_y, count):
+        return text.at[
+            place.along_z(dz),
+            pl.ds(first_y, count),
+            pl.ds(first_part + second_part, per_device - first_part - second_part),
+        ]
 
     z_up, z_down, y_up, y_down, y_on = {}, {}, {}, {}, {}
 
@@ -300,6 +307,8 @@
         y_on[dz, 1] = mail.push(block(1, dz, 1), block(1, dz, 1), place.to_y(-1))
 
     start_z(0)
+    own_last = last_rows(0, own_y, 1)
+    last_y = [mail.push(own_last, own_last, place.to_y(step)) for step in (1, 3, 2)]
     start_y(0, 0)
     own_order = orders.at[row]
     order_mail = [
@@ -475,6 +484,10 @@
     start_y(1, 1)
     mail.got(block(0, -1, 1), z_up[1])
     start_y(-1, 1)
+    for step, ticket in zip((1, 3, 2), last_y):
+        mail.got(last_rows(0, place.along_y(-step), 1), ticket)
+    last_up = mail.push(last_rows(0, 0, ring), last_rows(0, 0, ring), place.to_z(1))
+    last_down = mail.push(last_rows(0, 0, ring), last_rows(0, 0, ring), place.to_z(-1))
     spreads[1].last()
     spreads[2].last()
     spreads[3].forward()
@@ -515,6 +528,11 @@
     teacher.start()
     forward_y(-1)
     teacher.forward()
+    pair = ring // 2
+    mail.got(last_rows(-1, 0, ring), last_up)
+    last_up = mail.push(last_rows(-1, 0, pair), last_rows(-1, 0, pair), place.to_z(1))
+    mail.got(last_rows(1, 0, ring), last_down)
+    last_down = mail.push(last_rows(1, pair, pair), last_rows(1, pair, pair), place.to_z(-1))
     forward_y(1)
     end_y(-1)
     process(0, -1)
@@ -527,6 +545,8 @@
     process(1, -1)
     process(1, 1)
     end_y(2)
+    mail.got(last_rows(2, 0, pair), last_up)
+    mail.got(last_rows(2, pair, pair), last_down)
     process(0, 2)
     process(1, 2)
 
@@ -763,19 +783,9 @@
             mail.got(theirs, tickets[index, step])
             back[index, step] = mail.push(theirs, theirs, place.sibling())
 
-    def write(side):
-        for kind in range(kinds):
-            rows = pl.ds(pl.multiple_of((side * kinds + kind) * size, size), size)
-            for lane in range(pieces):
-                proj_out[rows, lane * size : (lane + 1) * size] = gathered[
-                    side, lane, kind
-                ].astype(jnp.float32)
-
-    write(core)
     for step in (0, 1, 3, 2):
         for index, (chosen, (own1, at1, to1), _) in enumerate(families):
             mail.got(gathered.at[other, at1(-step), chosen], back[index, step])
-    write(other)
     mail.finish()
 
 
@@ -802,12 +812,12 @@
     images = n_col * per_device
     hbm = pl.BlockSpec(memory_space=pl.ANY)
     vmem = pl.BlockSpec(memory_space=pltpu.VMEM)
-    copies = 230
-    grad_embed, grad_proj = pl.pallas_call(
+    copies = 236
+    grad_embed, gathered = pl.pallas_call(
         step_kernel,
         out_shape=(
             jax.ShapeDtypeStruct((per_device, width), f32),
-            jax.ShapeDtypeStruct((student_width, width), f32),
+            jax.ShapeDtypeStruct((2, pieces, kinds, size, size), bf16),
         ),
         in_specs=[hbm] * 8,
         out_specs=[vmem] * 2,
@@ -856,7 +866,6 @@
             pltpu.VMEM((kinds, size // 4, size), f32),
             pltpu.VMEM((ring - 1, kinds, 8, size), f32),
             pltpu.VMEM((2, kinds, size // 4, size), f32),
-            pltpu.VMEM((2, pieces, kinds, size, size), bf16),
             pltpu.SemaphoreType.DMA((8,)),
             pltpu.SemaphoreType.DMA((96,)),
             pltpu.SemaphoreType.DMA((copies,)),
@@ -874,7 +883,8 @@
         assignment,
         pair_ids,
     )
-    return grad_embed, grad_proj
+    grad_proj = gathered.transpose(0, 2, 3, 1, 4).reshape(student_width, width)
+    return grad_embed, grad_proj.astype(f32)
 
 
 def solution(mesh):

time: 168 us -> 165 us (0.982)
  Pallas kernels: 163 us -> 160 us
    pallas_call x1, Pallas kernels: 163 us -> 160 us  [body(): pl.pallas_call(step_kernel, out_shape=(jax.ShapeDtypeStruct((per_device,...]
    unnamed x2 -> x4, local copies, waits for them, and re-layouts: 4.34 us -> 1.97 us
where the time goes in v3:
time: 165 us
  Pallas kernels  160 us (97%)
  local copies, waits for them, and re-layouts  2.98 us (2%)
    pallas_call x1, Pallas kernels, body(): pl.pallas_call(step_kernel, out_shape=(jax.ShapeDtypeStruct((per_device,...  160 us

profile of v3, /device:TPU:1, one launch (start us, length us, event | category | flops | bytes accessed | tf_op | source)
XLA Modules:
  0.0 164.6 jit_solution(13737846272670113816)
XLA Ops:
  0.6 159.7 %shard_map.95 = (f32[128,512]{1,0:T(8,128)}, bf16[2,4,3,128,128]{4,3,2,1,0:T(8,128)(2,1)}) custom-call(bf16[128,768]{1,0:T(8,128)(2,1)} %si_hbm.1, bf16[768,512]{1,0:T(8,128)(2,1)} %sp_hbm.1, bf16[128,512]{1,0:T(8,128)(2,1)} %st_hbm.1, bf16[104,2048]{1,0:T(8,128)(2,1)} %bitcast.11, bf16[160,104]{1,0:T(8,128)(2,1)} %bitcast.12, bf16[128,1280]{1,0:T(8,128)(2,1)} %tt_hbm.1, ...), custom_call_target="tpu_custom_call" | custom-call | tf_op jit(solution)/shard_map/pallas_call | solution.py:816
  160.3 1.3 convert_bitcast_fusion
  161.6 1.0 copy.10
  162.6 0.0 copy-start
  162.6 1.3 copy.13
  163.9 0.0 copy-done
  163.9 0.7 copy.15
Async XLA Ops:
  162.6 1.3 copy-start

commit v4 on v3

--- a/solution.py
+++ b/solution.py
@@ -611,10 +611,11 @@
     over = {}
     across = {}
 
-    def weigh(step):
+    def weigh(step, first=0, last=ring):
         target = place.along_x(step)
         rows = pl.ds(pl.multiple_of(target * image_rows, image_rows), image_rows)
-        partial_grad[target] = jnp.zeros(partial_grad.shape[1:], jnp.float32)
+        if first == 0:
+            partial_grad[target] = jnp.zeros(partial_grad.shape[1:], jnp.float32)
 
         def texts(index, carry):
             parts = []
@@ -640,10 +641,11 @@
             partial_grad[target] += product.reshape(2, per_device, width)
             return carry
 
-        lax.fori_loop(0, ring, texts, 0)
-        over[step] = mail.push(
-            partial_grad.at[target, other], from_core.at[target], place.sibling()
-        )
+        lax.fori_loop(first, last, texts, 0)
+        if last == ring:
+            over[step] = mail.push(
+                partial_grad.at[target, other], from_core.at[target], place.sibling()
+            )
 
     def pass_over(step):
         target = place.along_x(step)
@@ -661,8 +663,9 @@
     pass_over(2)
     weigh(3)
     pass_over(1)
-    weigh(0)
+    weigh(0, 0, 3)
     pass_over(3)
+    weigh(0, 3, ring)
     embed_grad = pass_over(0)
     for step in (2, 1, 3):
         mail.got(arriving.at[step - 1], across[step])

time: 165 us -> 165 us (level)
  no operation moved by 1% of the time
where the time goes in v4:
time: 165 us
  Pallas kernels  160 us (97%)
  local copies, waits for them, and re-layouts  2.98 us (2%)
    pallas_call x1, Pallas kernels, body(): pl.pallas_call(step_kernel, out_shape=(jax.ShapeDtypeStruct((per_device,...  160 us

profile of v4, /device:TPU:1, one launch (start us, length us, event | category | flops | bytes accessed | tf_op | source)
XLA Modules:
  0.0 164.9 jit_solution(13663110414462389154)
XLA Ops:
  0.6 160.0 %shard_map.95 = (f32[128,512]{1,0:T(8,128)}, bf16[2,4,3,128,128]{4,3,2,1,0:T(8,128)(2,1)}) custom-call(bf16[128,768]{1,0:T(8,128)(2,1)} %si_hbm.1, bf16[768,512]{1,0:T(8,128)(2,1)} %sp_hbm.1, bf16[128,512]{1,0:T(8,128)(2,1)} %st_hbm.1, bf16[104,2048]{1,0:T(8,128)(2,1)} %bitcast.11, bf16[160,104]{1,0:T(8,128)(2,1)} %bitcast.12, bf16[128,1280]{1,0:T(8,128)(2,1)} %tt_hbm.1, ...), custom_call_target="tpu_custom_call" | custom-call | tf_op jit(solution)/shard_map/pallas_call | solution.py:819
  160.6 1.3 convert_bitcast_fusion
  161.9 1.0 copy.10
  162.9 0.0 copy-start
  162.9 1.3 copy.13
  164.2 0.0 copy-done
  164.2 0.7 copy.15
Async XLA Ops:
  162.9 1.3 copy-start
